TPU v7x, 256 devices: a whole 4x4x8 slice. The times are simulated.
256 devices in a mesh: ctx: 16 (over y_lo, z), tp: 8 (over x, core), role: 2 (over y_hi).
Axes of the slice: x: 4, y: 4 (y_hi: 2, y_lo: 2; y = y_hi * 2 + y_lo), z: 8, core: 2. Of those that a mesh axis runs over, the one named last changes fastest.
Arguments:
- token_ids: int32 [2, 2048], P('role', 'ctx'), may hold values from 0 to 65535
- embed_table: bfloat16 [65536, 7168], P(('ctx', 'role'), 'tp'), may hold values from -6 to 6
- latent_down: bfloat16 [7168, 576], P('tp'), may hold values from -0.0625 to 0.0625
- latent_gain: float32 [512], replicated, may hold values from 0.1 to 1.9
- prefill_query: bfloat16 [2048, 64, 576], P('ctx', 'tp'), may hold values from -120 to 120
- decode_query: bfloat16 [1024, 2, 64, 576], P(('ctx', 'tp')), may hold values from -120 to 120
- latent_cache: bfloat16 [1024, 512, 576], P(('ctx', 'tp')), may hold values from -6 to 6
- cache_length: int32 [1024], P(('ctx', 'tp')), may hold values from 1 to 512, as said below
- prompt_owner: int32 [2], replicated, may hold values from 0 to 15
Outputs:
- attended: bfloat16 [2, 2048, 32768], P('role', 'ctx', 'tp')
Inputs may be any that keep to these rules, and one draw needn't show every extreme that they name: `cache_length`: some row has exactly 512.
All inputs are finite; a program needn't handle non-finite values.
Results may differ from a plain program's by a relative error of at most 0.0099.
Values may be sent and summed in bfloat16 or wider, within the bound.
No kernel may reach another device: no remote copies, remote signals or barrier semaphores. Data moves between devices by JAX's collectives and lax.ppermute only.
A program may use at most 128 MiB of HBM per device.

v0:
```python
import jax
import jax.numpy as jnp
import numpy as np
from jax import lax
from jax.experimental import pallas as pl
from jax.experimental.pallas import tpu as pltpu
from jax.sharding import Mesh
from jax.sharding import PartitionSpec as P

LAT = 512
KVW = 576
STEPS = 2
WIDE = 640
SLOTS = 16
KEPT = 48
SIDE = 16 * KEPT
KEYS = 2048

score_scale = 0.07216878364870322
base_two = score_scale * 1.4426950408889634
masked_fill = -1e30
norm_eps = 1e-06
rope_base = 10000.0
bf16 = jnp.bfloat16
f32 = jnp.float32
SMEM = pltpu.SMEM
VMEM = pltpu.VMEM

HOLDERS = ("ylo", "z", "role")
PLANE = ("ylo", "role", "x")
TP = ("x", "core")


def iota(shape, axis):
    return lax.broadcasted_iota(jnp.int32, shape, axis)


def ones_where(flags):
    return jnp.where(flags, 1.0, 0.0).astype(bf16)


def dot(left, right):
    return lax.dot_general(left, right, (((1,), (0,)), ((), ())), preferred_element_type=f32)


def dot_nt(left, right):
    return lax.dot_general(left, right, (((1,), (1,)), ((), ())), preferred_element_type=f32)


def whole_loop(count, body, unroll=1):
    def step(index, carry):
        body(index)
        return carry

    lax.fori_loop(0, count, step, 0, unroll=unroll)


def aligned(index, size):
    return pl.ds(pl.multiple_of(index * size, size), size)


def spread_kernel(ids, out):
    out[...] = jnp.broadcast_to(ids[...].reshape(1, 1, 128), out.shape)


def select_kernel(place, ids, table, down, partial, hots, lows, chosen, table_here, down_here, sems):
    holder = (place[0] * 8 + place[1]) * 2 + place[4]
    table_copy = pltpu.make_async_copy(table, table_here, sems.at[0])
    down_copy = pltpu.make_async_copy(down, down_here, sems.at[1])
    table_copy.start()
    down_copy.start()

    def mark(line):
        tokens = ids[pl.ds(line, 1), :]
        span = aligned((line & 1) * 16 + (line >> 1), 128)
        hots[:, span] = ones_where(iota((16, 128), 0) == (tokens >> 7) - holder * 16)
        lows[:, span] = ones_where(iota((128, 128), 0) == (tokens & 127))

    whole_loop(32, mark, 8)
    in_prompt = dot_nt(hots[:, :KEYS], lows[:, :KEYS]) > 0.5
    alone = (dot_nt(hots[:, KEYS:], lows[:, KEYS:]) > 0.5) & jnp.logical_not(in_prompt)
    upper = ones_where(iota((128, 128), 0) < iota((128, 128), 1))
    all_ones = jnp.ones((128, 128), bf16)
    row = iota((8 * SLOTS, 128), 0)
    wanted = ((row & 15) * 8 + (((row >> 4) - holder) & 7)).astype(f32)
    before = jnp.zeros((1, 128), f32)
    ranks = []
    for present in (in_prompt, alone):
        flags = ones_where(present)
        within = dot(flags, upper)
        totals = dot(flags, all_ones)
        lines = []
        for step in range(16):
            lines.append(within[step : step + 1, :] + before)
            before = before + totals[step : step + 1, :]
        ranks.append(lines)
    for step in range(16):
        rank = jnp.where(alone[step : step + 1, :], ranks[1][step], -1.0)
        rank = jnp.where(in_prompt[step : step + 1, :], ranks[0][step], rank)
        chosen[:, step * 128 : (step + 1) * 128] = ones_where(wanted == rank)
    table_copy.wait()
    rows = dot(chosen[...], table_here[...]).astype(bf16)
    down_copy.wait()
    partial[...] = dot_nt(rows, down_here[...]).reshape(partial.shape)


def rank_kernel(ids, sheet, highs, lows):
    square = (128, 128)
    lane = iota((8, 128), 1)
    sheet[0:16, :] = ids[pl.ds(0, 16, stride=2), :]
    sheet[16:32, :] = ids[pl.ds(1, 16, stride=2), :]
    target = iota(square, 1)
    mover = ones_where(iota(square, 0) == jnp.where(target < 64, 2 * target, 2 * target - 127))
    plain = sheet[0:16, :]
    decode_tokens = sheet[16:32, :]
    coarse = (plain >> 8).astype(f32).astype(bf16)
    fine = (plain & 255).astype(f32).astype(bf16)
    moved = dot(coarse, mover) * 256.0 + dot(fine, mover)
    sheet[0:16, :] = moved.astype(jnp.int32)
    even = sheet[pl.ds(0, 8, stride=2), :]
    odd = sheet[pl.ds(1, 8, stride=2), :]
    first = jnp.where(lane < 64, even, pltpu.roll(odd, 64, 1))
    second = jnp.where(lane < 64, pltpu.roll(even, 64, 1), odd)
    tokens = jnp.concatenate([first, second, decode_tokens], axis=0)
    sheet[0:32, :] = tokens

    def mark(block):
        line = sheet[pl.ds(block, 1), :]
        span = aligned(block, 128)
        highs[:, span] = ones_where(iota((512, 128), 0) == (line >> 7))
        lows[:, span] = ones_where(iota(square, 0) == (line & 127))

    whole_loop(32, mark, 8)
    in_prompt = dot_nt(lows[:, :KEYS], highs[:, :KEYS]) > 0.5
    alone = (dot_nt(lows[:, KEYS:], highs[:, KEYS:]) > 0.5) & jnp.logical_not(in_prompt)
    below = ones_where(iota(square, 1) < iota(square, 0))
    all_ones = jnp.ones(square, bf16)
    wide = (512, 512)
    same = (iota(wide, 0) >> 4) == (iota(wide, 1) >> 4)
    in_holder = ones_where(same & (iota(wide, 0) < iota(wide, 1)))
    prompt_flags = ones_where(in_prompt)
    alone_flags = ones_where(alone)
    prompt_columns = dot(all_ones, prompt_flags).astype(bf16)
    alone_columns = dot(all_ones, alone_flags).astype(bf16)
    prompt_rank = dot(below, prompt_flags) + dot(prompt_columns, in_holder)
    alone_rank = (
        dot(below, alone_flags) + dot(alone_columns, in_holder) + dot(prompt_columns, ones_where(same))
    )
    rank = jnp.where(in_prompt, prompt_rank, jnp.where(alone, alone_rank, 0.0))
    top_rank = jnp.max(jnp.max(rank, axis=0, keepdims=True), axis=1, keepdims=True).astype(jnp.int32)
    coded = (jnp.minimum(rank, 127.0) + jnp.where(in_prompt, 128.0, 0.0)).astype(bf16)
    pieces = []
    for chunk in range(4):
        span = slice(chunk * 1024, (chunk + 1) * 1024)
        looked = dot(coded, highs[:, span]) * lows[:, span].astype(f32)
        line = jnp.sum(looked, axis=0, keepdims=True)
        for part in range(8):
            pieces.append(line[:, part * 128 : (part + 1) * 128])
    value = jnp.concatenate(pieces, axis=0).astype(jnp.int32)
    ranks = value & 127
    holder = tokens >> 11
    tp_of = (ranks + holder) & 7
    quad = tp_of * 16 + (ranks >> 3)
    sheet[0:32, :] = quad
    sheet[32:64, :] = holder
    sheet[64:96, :] = jnp.where(value >= 128, -1, tp_of)
    sheet[96:104, :] = jnp.broadcast_to(top_rank, (8, 128))


def place_kernel(place, sheet, columns, kept, fits, quads, holders, hot_tp, hot_pool, sheet_b):
    ylo, zed, ex, core, section = place[0], place[1], place[2], place[3], place[4]
    square = (128, 128)

    def spot(block, source):
        span = aligned(block, 128)
        quads[:, span] = ones_where(iota(square, 0) == sheet[pl.ds(source, 1), :])
        holders[:, span] = ones_where(iota(square, 0) == sheet[pl.ds(source + 32, 1), :])

    whole_loop(16, lambda block: spot(block, block), 8)
    for part in range(2):
        spot(16 + part, 16 + part * 8 + zed)
    own = 16 + ylo * 8 + zed
    spot(18, own)
    up, down = iota(square, 0), iota(square, 1)
    same_tp = (up >> 4) == (down >> 4)
    same_pool = ((up >> 4) == (down >> 4)) & ((up & 1) == (down & 1))
    tp_ones = ones_where(same_tp)
    pool = ones_where(same_pool)
    before = ones_where(same_pool & (up < down))
    in_tp = ones_where(same_tp & (down < up))
    held = dot_nt(quads[:, :KEYS], holders[:, :KEYS]) > 0.5
    flags = ones_where(held)
    sums = dot(tp_ones, flags).astype(bf16)
    prompt_position = dot(in_tp, flags) + dot(sums, before)
    prompt_count = dot(sums, pool)
    positions = []
    for part in range(2):
        span = slice(KEYS + part * 128, KEYS + (part + 1) * 128)
        added = (dot_nt(quads[:, span], holders[:, span]) > 0.5) & jnp.logical_not(held)
        added_flags = ones_where(added)
        added_sums = dot(tp_ones, added_flags).astype(bf16)
        spots = dot(in_tp, added_flags) + dot(added_sums, before) + prompt_count
        spots = jnp.where(held, prompt_position, jnp.where(added, spots, 255.0))
        positions.append(jnp.minimum(spots, 255.0))
    position = jnp.where(ylo == 0, positions[0], positions[1])

    def pick(block):
        span = aligned(block, 128)
        hot_tp[:, span] = ones_where(iota((16, 128), 0) == sheet[pl.ds(block + 80, 1), :])
        line = sheet[pl.ds(block + 48, 1), :]
        line = ((line >> 4) * 2 + (line & 1)) + 4 * block
        hot_pool[:, span] = ones_where(iota((64, 128), 0) == line)

    whole_loop(16, pick, 8)
    gather_tp = ones_where(iota((16, 128), 0) == (iota((16, 128), 1) >> 4))
    base = dot(gather_tp, flags).astype(bf16)
    holder, column = iota((128, 64), 0), iota((128, 64), 1)
    pooled = ones_where((holder < 32) & (((holder >> 4) * 2 + (holder & 1)) == (column & 3)))
    needed = dot_nt(hot_tp[...], hot_pool[...]) + dot(base, pooled)
    needed = jnp.max(jnp.max(needed, axis=0, keepdims=True), axis=1, keepdims=True)
    enough = (sheet[96:97, 0:1] < 8 * SLOTS) & (needed <= float(KEPT))
    fits[0, 0] = jnp.max(jnp.where(enough, 1, 0))

    looked = dot(position.astype(bf16), holders[...]) * quads[...].astype(f32)
    line = jnp.sum(looked, axis=0, keepdims=True)
    found = [line[:, block * 128 : (block + 1) * 128] for block in range(19)]
    found = jnp.concatenate(found + [jnp.zeros((5, 128), f32)], axis=0)
    blank = jnp.zeros((5, 128), jnp.int32)
    quad_rows = jnp.concatenate([sheet[0:16, :], blank[:2], sheet[pl.ds(own, 1), :], blank], axis=0)
    holder_rows = jnp.concatenate([sheet[32:48, :], blank[:2], sheet[pl.ds(own + 32, 1), :], blank], axis=0)
    tp_rows = quad_rows >> 4
    source = ((holder_rows >> 4) * 2 + (holder_rows & 1)) * 4 + (tp_rows >> 1)
    side = jnp.where((tp_rows & 1) == core, 0, SIDE)
    final = found + (source * KEPT + side).astype(f32)
    tp_index = ex * 2 + core
    turned = pltpu.roll(final, (128 - tp_index * 16) % 128, 1)
    turned = jnp.where(iota((24, 128), 1) < 16, turned, -1.0)
    final = jnp.where(iota((24, 128), 0) == 18, turned, final)
    final = jnp.concatenate([final, jnp.zeros((104, 128), f32)], axis=0)
    columns[...] = jnp.transpose(final).astype(jnp.int32)
    few = (16, 128)
    for part in range(2):
        sheet_b[...] = positions[part]
        mine = sheet_b[pl.ds(pl.multiple_of(tp_index * 16, 16), 16), :].astype(bf16)
        spread = dot(mine, ones_where(up == (ylo * 8 + (down >> 4)) * 2 + section))
        spread = jnp.where((iota(few, 1) & 15) == iota(few, 0), spread, 0.0)
        kept[part : part + 1, :] = jnp.sum(spread, axis=0, keepdims=True)


def finish_kernel(parts, gain, sent):
    latent = parts[0]
    for tp in range(1, parts.shape[0]):
        latent = latent + parts[tp]
    plain = latent[:, :LAT]
    scaled = plain * lax.rsqrt(jnp.mean(plain * plain, axis=-1, keepdims=True) + norm_eps) * gain[...]
    rotary = latent[:, LAT:]
    coarse = rotary.astype(bf16)
    fine = (rotary - coarse.astype(f32)).astype(bf16)
    row = jnp.concatenate([scaled.astype(bf16), coarse, fine], axis=-1)
    for peer in range(sent.shape[0]):
        sent[peer] = row


def keep_kernel(kept, rows, sent):
    for ylo in range(2):
        chosen = iota((KEPT, 128), 0).astype(f32) == kept[ylo : ylo + 1, :]
        row = dot(ones_where(chosen), rows[...]).astype(bf16)
        for peer in range(8):
            sent[ylo * 8 + peer] = row


def cache_kernel(lengths, query, cache, out, level):
    length = lengths[pl.program_id(0)]
    scores = dot(query[0], cache[0]) * base_two
    scores = jnp.where(iota(scores.shape, 1) < length, scores, masked_fill)
    highest = jnp.max(scores, axis=-1, keepdims=True)
    weights = jnp.exp2(scores - highest)
    total = jnp.sum(weights, axis=-1, keepdims=True)
    out[...] = (dot_nt(weights.astype(bf16), cache[0, :LAT, :]) * (1.0 / total)).astype(bf16)
    level[...] = jnp.broadcast_to(highest + jnp.log2(total), level.shape)


def hot_rows(hot, columns, prompt, side):
    turned = pltpu.roll(columns[...], (128 - prompt * 8) % 128, 1) - side * SIDE
    for block in range(8):
        hot[block * 128 : (block + 1) * 128, :] = ones_where(iota((128, SIDE), 1) == turned[:, block : block + 1])


def empty_kernel(*refs):
    pass


def fresh_hot(columns, side):
    return ones_where(iota((128, SIDE), 1) == columns[:, 18:19] - side * SIDE)


def put_keys(keys, span, found, factor):
    turning = found[:, LAT:]
    turning = turning + pltpu.roll(turning, 64, 1)
    turned = turning * factor + pltpu.roll(turning, 32, 1) * pltpu.roll(factor, 64, 1)
    keys[span, :LAT] = found[:, :LAT].astype(bf16)
    keys[span, LAT:] = turned[:, : KVW - LAT].astype(bf16)


def copy_in(source, target, sem):
    copy = pltpu.make_async_copy(source, target, sem)
    copy.start()
    copy.wait()


def weigh(scores, old):
    new = jnp.maximum(old, jnp.max(scores, axis=-1, keepdims=True))
    weights = jnp.exp2(scores - new)
    return new, jnp.exp2(old - new), jnp.sum(weights, axis=-1, keepdims=True), weights.astype(bf16)


def near_kernel(place, owner, slots, columns, near, hot):
    group = place[0] * 8 + place[1]

    @pl.when(place[4] == 1)
    def _():
        near[KEYS : KEYS + 128, :] = dot(fresh_hot(columns, 0), slots[...]).astype(bf16)

    def open_prompt(prompt):
        @pl.when((place[4] == 0) | (owner[prompt] == group))
        def _():
            hot_rows(hot, columns, prompt, 0)

            def open_part(part):
                near[aligned(prompt * 2 + part, 512), :] = dot(hot[aligned(part, 512), :], slots[...]).astype(bf16)

            whole_loop(2, open_part, 2)

    whole_loop(2, open_prompt)


def decode_kernel(
    place, owner, fits, near, others, columns, new_factors, factors_far, query_far, earlier_far, level_far, spare, spare_new,
    out, out_here, factors, query, earlier, level, keys, hot, highest, total, mixed, sem, in_sems, out_sems
):
    group = place[0] * 8 + place[1]
    fitting = fits[0, 0] == 1

    @pl.when(place[4] == 1)
    def _():
        loads = [
            pltpu.make_async_copy(source, target, in_sems.at[index])
            for index, (source, target) in enumerate(
                ((factors_far, factors), (query_far, query), (level_far, level), (earlier_far, earlier))
            )
        ]
        for load in loads:
            load.start()

        @pl.when(fitting)
        def _():
            span = slice(KEYS, KEYS + 128)
            found = near[span, :].astype(f32) + dot(fresh_hot(columns, 1), others[...])
            put_keys(keys, span, found, new_factors[...])

        @pl.when(jnp.logical_not(fitting))
        def _():
            copy_in(spare_new, keys.at[pl.ds(KEYS, 128)], sem)

        loads[0].wait()

        def open_prompt(prompt):
            owned = owner[prompt] == group

            @pl.when(owned & fitting)
            def _():
                hot_rows(hot, columns, prompt, 1)

                def open_part(part):
                    span = aligned(prompt * 2 + part, 512)
                    found = near[span, :].astype(f32) + dot(hot[aligned(part, 512), :], others[...])
                    put_keys(keys, span, found, factors[aligned(part, 512), :])

                whole_loop(2, open_part, 2)

            @pl.when(owned & jnp.logical_not(fitting))
            def _():
                copy_in(spare.at[pl.ds(prompt * 1024, 1024)], keys.at[pl.ds(prompt * 1024, 1024)], sem)

        whole_loop(2, open_prompt)
        for load in loads[1:]:
            load.wait()
        newest = keys[KEYS : KEYS + 128, :]

        def begin(piece):
            span = aligned(piece, 256)
            scores = dot_nt(query[span, :], newest) * base_two
            key = iota(scores.shape, 1)
            row = iota(scores.shape, 0) & 15
            allowed = ((key >> 1) == (row >> 1)) & ((key & 1) <= (row & 1))
            scores = jnp.where(allowed, scores, masked_fill)
            new, factor, summed, weights = weigh(scores, level[span, 0:1])
            mixed[span, :] = earlier[span, :].astype(f32) * factor + dot(weights, newest[:, :LAT])
            highest[span, :] = jnp.broadcast_to(new, (256, 128))
            total[span, :] = jnp.broadcast_to(factor + summed, (256, 128))

        whole_loop(4, begin, 4)

        def add_prompt(prompt):
            @pl.when(owner[prompt] == group)
            def _():
                def add_part(piece):
                    span = aligned(piece, 256)
                    some = keys[aligned(prompt, 1024), :]
                    new, factor, summed, weights = weigh(dot_nt(query[span, :], some) * base_two, highest[span, 0:1])
                    mixed[span, :] = mixed[span, :] * factor + dot(weights, some[:, :LAT])
                    highest[span, :] = jnp.broadcast_to(new, (256, 128))
                    total[span, :] = total[span, :] * factor + summed

                whole_loop(4, add_part, 4)

        whole_loop(2, add_prompt)

        def out_copy(tp):
            rows = aligned(tp, 16)
            return pltpu.make_async_copy(out_here.at[rows], out.at[rows], out_sems.at[tp])

        def tp_rows(tp):
            for head in range(8):
                rows = pl.ds(pl.multiple_of(tp * 128 + head * 16, 16), 16)
                some = mixed[rows, :] * (1.0 / total[rows, 0:1])
                out_here[aligned(tp, 16), head * LAT : (head + 1) * LAT] = some.astype(bf16)
            out_copy(tp).start()

        whole_loop(8, tp_rows, 2)
        whole_loop(8, lambda tp: out_copy(tp).wait())


def prefill_kernel(place, fits, near, others, columns, factors, query, spare, out, keys, hot, mixed, pairs, sem):
    group = place[0] * 8 + place[1]
    fitting = fits[0, 0] == 1

    @pl.when(place[4] == 0)
    def _():
        def add_prompt(prompt):
            @pl.when(fitting)
            def _():
                hot_rows(hot, columns, prompt, 1)

                def open_part(part):
                    span = aligned(part, 512)
                    found = near[aligned(prompt * 2 + part, 512), :].astype(f32) + dot(hot[span, :], others[...])
                    put_keys(keys, span, found, factors[span, :])

                whole_loop(2, open_part, 2)

            @pl.when(jnp.logical_not(fitting))
            def _():
                copy_in(spare.at[pl.ds(prompt * 1024, 1024)], keys, sem)

            span = aligned(prompt, 512)
            some = keys[...]
            scores = dot_nt(query[span, :], some) * base_two
            last = (iota((512, 1), 0) & 63) + group * 64
            scores = jnp.where(iota(scores.shape, 1) <= last, scores, masked_fill)
            _, _, summed, weights = weigh(scores, jnp.full((512, 1), masked_fill, f32))
            added = dot(weights, some[:, :LAT]) * (1.0 / summed)
            for column in range(4):
                mixed[column, span, :] = added[:, column * 128 : (column + 1) * 128]

        whole_loop(2, add_prompt)

        def head_rows(head):
            for column in range(4):
                for prompt in range(2):
                    start = pl.multiple_of(prompt * 512 + head * 64, 64)
                    pairs[column, pl.ds(prompt, 64, stride=2), :] = mixed[column, pl.ds(start, 64), :]
                out[:, pl.ds(pl.multiple_of(head * LAT + column * 128, 128), 128)] = pairs[column].astype(bf16)

        whole_loop(8, head_rows, 2)


def join_kernel(place, prefilled, turned, out, sems):
    @pl.when(place[4] == 1)
    def _():
        copies = []
        for part in range(4):
            span = pl.ds(part * 32, 32)
            copies.append(pltpu.make_async_copy(turned.at[span], out.at[span], sems.at[part]))
        for copy in copies:
            copy.start()
        for copy in copies:
            copy.wait()


def rope_factors(position):
    frequency = np.float32(rope_base) ** (-np.arange(32, dtype=np.float32) / np.float32(32))
    angles = position[:, None] * frequency[None, :]
    if isinstance(position, np.ndarray):
        angles = angles.astype(np.float32).astype(np.float64)
        cosine, sine = np.cos(angles), np.sin(angles)
        return np.concatenate([cosine, cosine, -sine, sine], axis=-1).astype(np.float32)
    cosine, sine = jnp.cos(angles), jnp.sin(angles)
    return jnp.concatenate([cosine, cosine, -sine, sine], axis=-1)


def finish_keys(latent, latent_gain, position):
    plain = latent[:, :LAT]
    scaled = plain * lax.rsqrt(jnp.mean(plain * plain, axis=-1, keepdims=True) + norm_eps) * latent_gain
    factors = rope_factors(position.astype(f32))
    rotary = latent[:, LAT:]
    swapped = jnp.concatenate([rotary[:, 32:], rotary[:, :32]], axis=-1)
    turned = rotary * factors[:, :64] + swapped * factors[:, 64:]
    return jnp.concatenate([scaled, turned], axis=-1).astype(bf16)


def dense_keys(token_ids, place, embed_table, down, latent_gain, cache_length):
    group = place[0] * 8 + place[1]
    tp_index = place[2] * 2 + place[3]
    every = lax.all_to_all(jnp.broadcast_to(token_ids, (32, 128)).reshape(32, 1, 128), HOLDERS, 0, 0, tiled=True)
    local_row = every.reshape(-1) - (group * 2 + place[4]) * 2048
    inside = (local_row >= 0) & (local_row < 2048)
    picked = jnp.take(embed_table, jnp.clip(local_row, 0, 2047), axis=0)
    picked = jnp.where(inside[:, None], picked, jnp.zeros_like(picked)).reshape(32, 128, 896)
    embedded = jnp.sum(lax.all_to_all(picked, HOLDERS, 0, 0, tiled=True).astype(f32), axis=0).astype(bf16)
    partial = dot_nt(embedded, down)
    spread = jnp.broadcast_to(partial[None], (8, 128, KVW))
    latent = jnp.sum(lax.all_to_all(spread, TP, 0, 0, tiled=True), axis=0)
    index = jnp.arange(128, dtype=jnp.int32)
    mine = finish_keys(latent, latent_gain, group * 64 + index // 2)
    spread = jnp.broadcast_to(mine[None], (32, 128, KVW))
    prompts = lax.all_to_all(spread, HOLDERS, 0, 0, tiled=True).reshape(16, 2, 64, 2, KVW)[:, 0]
    prompts = jnp.transpose(prompts, (2, 0, 1, 3)).reshape(KEYS, KVW)
    own = lax.dynamic_slice_in_dim(latent, tp_index * 16, 16, 0)
    fresh = finish_keys(own, latent_gain, (cache_length[:, None] + jnp.arange(2, dtype=jnp.int32)[None]).reshape(-1))
    return prompts, jnp.concatenate([fresh, jnp.zeros((112, KVW), bf16)], axis=0)


def in_vmem(value):
    return pltpu.with_memory_space_constraint(value, VMEM)


def in_hbm(value):
    return pltpu.with_memory_space_constraint(value, pltpu.HBM)


def params(mebibytes):
    return pltpu.CompilerParams(vmem_limit_bytes=mebibytes * 1024 * 1024)


def shards(
    token_ids,
    embed_table,
    latent_down,
    latent_gain,
    prefill_query,
    decode_query,
    latent_cache,
    cache_length,
    prompt_owner,
):
    place = jnp.stack([lax.axis_index(name) for name in ("ylo", "z", "x", "core", "role")]).astype(jnp.int32)
    down = jnp.transpose(latent_down)
    whole = pl.BlockSpec(memory_space=VMEM)
    scalars = pl.BlockSpec(memory_space=SMEM)
    anywhere = pl.BlockSpec(memory_space=pl.ANY)
    shaped = jax.ShapeDtypeStruct

    spread = pl.pallas_call(
        spread_kernel,
        out_shape=shaped((32, 1, 128), jnp.int32),
        in_specs=[whole],
        out_specs=whole,
        compiler_params=params(4),
        name="spread_ids",
    )(token_ids)
    every = lax.all_to_all(spread, HOLDERS, 0, 0, tiled=True).reshape(32, 128)

    earlier, level = pl.pallas_call(
        cache_kernel,
        grid_spec=pltpu.PrefetchScalarGridSpec(
            num_scalar_prefetch=1,
            grid=(8,),
            in_specs=[
                pl.BlockSpec((1, 128, KVW), lambda row, lengths: (row, 0, 0)),
                pl.BlockSpec((1, KVW, 512), lambda row, lengths: (row, 0, 0)),
            ],
            out_specs=[
                pl.BlockSpec((128, LAT), lambda row, lengths: (row, 0)),
                pl.BlockSpec((128, 128), lambda row, lengths: (row, 0)),
            ],
        ),
        out_shape=(pltpu.HBM((1024, LAT), bf16), pltpu.HBM((1024, 128), f32)),
        compiler_params=params(12),
        cost_estimate=pl.CostEstimate(flops=12 * 10**8, bytes_accessed=7 * 10**6, transcendentals=524288),
        name="cache_rows",
    )(cache_length, in_hbm(decode_query.reshape(8, 128, KVW)), in_hbm(jnp.swapaxes(latent_cache, 1, 2)))
    every, earlier, level = lax.optimization_barrier((every, earlier, level))

    partial = pl.pallas_call(
        select_kernel,
        out_shape=shaped((8, SLOTS, KVW), f32),
        in_specs=[scalars, whole, anywhere, anywhere],
        out_specs=whole,
        scratch_shapes=[
            VMEM((16, 4096), bf16),
            VMEM((128, 4096), bf16),
            VMEM((8 * SLOTS, 2048), bf16),
            VMEM((2048, 896), bf16),
            VMEM((KVW, 896), bf16),
            pltpu.SemaphoreType.DMA((2,)),
        ],
        compiler_params=params(16),
        cost_estimate=pl.CostEstimate(flops=3 * 10**9, bytes_accessed=5 * 10**6, transcendentals=0),
        name="select_rows",
    )(place, every, in_hbm(embed_table), in_hbm(down))
    parts = lax.all_to_all(partial, TP, 0, 0, tiled=True)

    sheet = pl.pallas_call(
        rank_kernel,
        out_shape=shaped((104, 128), jnp.int32),
        in_specs=[whole],
        out_specs=whole,
        scratch_shapes=[VMEM((512, 4096), bf16), VMEM((128, 4096), bf16)],
        compiler_params=params(18),
        cost_estimate=pl.CostEstimate(flops=2 * 10**9, bytes_accessed=10**6, transcendentals=0),
        name="rank_rows",
    )(every)
    parts, sheet = lax.optimization_barrier((parts, sheet))
    sent = pl.pallas_call(
        finish_kernel,
        out_shape=shaped((8, SLOTS, WIDE), bf16),
        in_specs=[whole, whole],
        out_specs=whole,
        compiler_params=params(8),
        name="finish_rows",
    )(parts, latent_gain.reshape(1, LAT))
    arrived = lax.all_to_all(sent, "z", 0, 0, tiled=True)

    columns, kept, fits = pl.pallas_call(
        place_kernel,
        out_shape=(shaped((128, 128), jnp.int32), shaped((8, 128), f32), shaped((1, 1), jnp.int32)),
        in_specs=[scalars, whole],
        out_specs=(whole, whole, scalars),
        scratch_shapes=[
            VMEM((128, 19 * 128), bf16),
            VMEM((128, 19 * 128), bf16),
            VMEM((16, 2048), bf16),
            VMEM((64, 2048), bf16),
            VMEM((128, 128), f32),
        ],
        compiler_params=params(12),
        cost_estimate=pl.CostEstimate(flops=10**9, bytes_accessed=10**6, transcendentals=0),
        name="place_rows",
    )(place, sheet)
    handed = pl.pallas_call(
        keep_kernel,
        out_shape=shaped((16, KEPT, WIDE), bf16),
        in_specs=[whole] * 2,
        out_specs=whole,
        compiler_params=params(8),
        name="keep_rows",
    )(kept, arrived.reshape(8 * SLOTS, WIDE))
    handed, prompt_rows, decode_rows, lengths, earlier, level = lax.optimization_barrier(
        (handed, prefill_query, decode_query, cache_length, earlier, level)
    )
    slots = lax.all_to_all(handed, PLANE, 0, 0, tiled=True).reshape(SIDE, WIDE)

    def by_head(rows):
        return jnp.transpose(rows.reshape(16, 64, -1), (1, 0, 2)).reshape(1024, -1)

    row_query, earlier, level = by_head(decode_rows), by_head(earlier), by_head(level)
    new_position = (lengths[:, None] + jnp.arange(2, dtype=jnp.int32)[None]).reshape(-1)
    new_factors = jnp.pad(rope_factors(new_position.astype(f32)), ((0, 112), (0, 0)))
    prompt_query = jnp.transpose(prompt_rows.reshape(64, 2, 8, KVW), (1, 2, 0, 3)).reshape(1024, KVW)
    slots, prompt_query, row_query, earlier, level, new_factors = lax.optimization_barrier(
        (slots, prompt_query, row_query, earlier, level, new_factors)
    )
    others = lax.ppermute(slots, "core", [(0, 1), (1, 0)])

    spare, spare_new = lax.cond(
        fits[0, 0] == 1,
        lambda *unused: tuple(
            pl.pallas_call(
                empty_kernel,
                out_shape=[shaped((KEYS, KVW), bf16), shaped((128, KVW), bf16)],
                out_specs=[anywhere] * 2,
                name="no_keys",
            )()
        ),
        dense_keys,
        token_ids,
        place,
        embed_table,
        down,
        latent_gain,
        cache_length,
    )

    near = pl.pallas_call(
        near_kernel,
        out_shape=VMEM((KEYS + 128, WIDE), bf16),
        in_specs=[scalars, scalars, whole, whole],
        out_specs=whole,
        scratch_shapes=[VMEM((1024, SIDE), bf16)],
        compiler_params=params(12),
        cost_estimate=pl.CostEstimate(flops=2 * 10**9, bytes_accessed=10**6, transcendentals=0),
        name="near_keys",
    )(place, prompt_owner, slots, columns)
    factors = jnp.asarray(rope_factors(np.arange(1024, dtype=np.float32)))
    decoded = pl.pallas_call(
        decode_kernel,
        out_shape=pltpu.HBM((128, 4096), bf16),
        in_specs=[scalars] * 3 + [whole] * 4 + [anywhere] * 6,
        out_specs=anywhere,
        scratch_shapes=[
            VMEM((128, 4096), bf16),
            VMEM((1024, 128), f32),
            VMEM((1024, KVW), bf16),
            VMEM((1024, LAT), bf16),
            VMEM((1024, 128), f32),
            VMEM((KEYS + 128, KVW), bf16),
            VMEM((1024, SIDE), bf16),
            VMEM((1024, 128), f32),
            VMEM((1024, 128), f32),
            VMEM((1024, LAT), f32),
            pltpu.SemaphoreType.DMA,
            pltpu.SemaphoreType.DMA((4,)),
            pltpu.SemaphoreType.DMA((8,)),
        ],
        compiler_params=params(24),
        cost_estimate=pl.CostEstimate(flops=5 * 10**9, bytes_accessed=7 * 10**6, transcendentals=10**6),
        name="decode_rows",
    )(
        place, prompt_owner, fits, in_vmem(near), in_vmem(others), columns, new_factors, in_hbm(factors),
        in_hbm(row_query), in_hbm(earlier), in_hbm(level), in_hbm(spare), in_hbm(spare_new),
    )
    turned = lax.all_to_all(decoded.reshape(8, 16, 4096), TP, 0, 0, tiled=True).reshape(128, 4096)
    prefilled = pl.pallas_call(
        prefill_kernel,
        out_shape=pltpu.HBM((128, 4096), bf16),
        in_specs=[scalars] * 2 + [whole] * 5 + [anywhere],
        out_specs=whole,
        scratch_shapes=[
            VMEM((1024, KVW), bf16),
            VMEM((1024, SIDE), bf16),
            VMEM((4, 1024, 128), f32),
            VMEM((4, 128, 128), f32),
            pltpu.SemaphoreType.DMA,
        ],
        compiler_params=params(20),
        cost_estimate=pl.CostEstimate(flops=7 * 10**9, bytes_accessed=7 * 10**6, transcendentals=10**6),
        name="prefill_rows",
    )(place, fits, in_vmem(near), in_vmem(others), columns, in_vmem(factors), in_vmem(prompt_query), in_hbm(spare))
    out = pl.pallas_call(
        join_kernel,
        out_shape=pltpu.HBM((128, 4096), bf16),
        in_specs=[scalars] + [anywhere] * 2,
        out_specs=anywhere,
        scratch_shapes=[pltpu.SemaphoreType.DMA((4,))],
        input_output_aliases={1: 0},
        compiler_params=params(4),
        name="join_rows",
    )(place, in_hbm(prefilled), turned)
    return out[None]


def solution(mesh):
    fine_mesh = Mesh(mesh.devices.reshape(2, 8, 4, 2, 2), ("ylo", "z", "x", "core", "role"))
    ctx, tp = ("ylo", "z"), ("x", "core")
    in_specs = (
        P("role", ctx),
        P(ctx + ("role",), tp),
        P(tp, None),
        P(),
        P(ctx, tp, None),
        P(ctx + tp, None, None, None),
        P(ctx + tp, None, None),
        P(ctx + tp),
        P(),
    )
    out_specs = P("role", ctx, tp)
    return jax.shard_map(shards, mesh=fine_mesh, in_specs=in_specs, out_specs=out_specs, check_vma=False)
```

profile of v0, /device:TPU:56, one launch (start us, length us, event | category | flops | bytes accessed | tf_op | source)
XLA Modules:
  0.0 111.0 jit_solution(10997486374795731018)
XLA Ops:
  0.0 1.3 %spread_ids.1 = s32[32,1,128]{2,1,0:T(1,128)} custom-call(s32[1,128]{1,0:T(1,128)} %ids.1), custom_call_target="tpu_custom_call" | custom-call | tf_op jit(solution)/shard_map/spread_ids/pallas_call | solution.py:564
  1.3 11.0 %all-to-all-start.4 = ((s32[32,1,128]{2,1,0:T(1,128)}), s32[32,1,128]{2,1,0:T(1,128)S(1)}, u32[]{:S(2)}, u32[]{:S(2)}) async-start(s32[32,1,128]{2,1,0:T(1,128)} %spread_ids.1), calls=%async_computation.4 | async-start | bytes 32768 | tf_op jit(solution)/shard_map/all_to_all | solution.py:572
  12.3 9.1 %cache_rows.1 = (bf16[1024,512]{1,0:T(8,128)(2,1)}, f32[1024,128]{1,0:T(8,128)}) custom-call(s32[8]{0:T(128)} %lengths.1, bf16[8,128,576]{2,1,0:T(8,128)(2,1)} %bitcast.61, bf16[8,576,512]{2,1,0:T(8,128)(2,1)} %bitcast.63), custom_call_target="tpu_custom_call" | custom-call | flops 1200000000 | bytes 7000000 | tf_op jit(solution)/shard_map/cache_rows/pallas_call | solution.py:574
  21.4 0.1 stack.23.place
  21.5 4.6 %select_rows.1 = f32[8,16,576]{2,1,0:T(8,128)} custom-call(s32[5]{0:T(128)S(1)} %stack.23.place, s32[32,128]{1,0:T(8,128)S(1)} %bitcast.57, bf16[2048,896]{1,0:T(8,128)(2,1)} %table.1, bf16[576,896]{1,0:T(8,128)(2,1)} %bitcast.69), custom_call_target="tpu_custom_call" | custom-call | flops 3000000000 | bytes 5000000 | tf_op jit(solution)/shard_map/select_rows/pallas_call | solution.py:595
  26.1 4.3 %all-to-all-start.5 = ((f32[8,16,576]{2,1,0:T(8,128)}), f32[8,16,576]{2,1,0:T(8,128)S(1)}, u32[]{:S(2)}, u32[]{:S(2)}) async-start(f32[8,16,576]{2,1,0:T(8,128)} %select_rows.1), calls=%async_computation.5 | async-start | bytes 655360 | tf_op jit(solution)/shard_map/all_to_all | solution.py:612
  30.4 4.9 %rank_rows.1.sheet = s32[104,128]{1,0:T(8,128)S(1)} custom-call(s32[32,128]{1,0:T(8,128)S(1)} %bitcast.58), custom_call_target="tpu_custom_call" | custom-call | flops 2000000000 | bytes 1000000 | tf_op jit(solution)/shard_map/rank_rows/pallas_call | solution.py:614
  35.3 3.3 %all-to-all-done.5.parts = f32[8,16,576]{2,1,0:T(8,128)S(1)} async-done(((f32[8,16,576]{2,1,0:T(8,128)}), f32[8,16,576]{2,1,0:T(8,128)S(1)}, u32[]{:S(2)}, u32[]{:S(2)}) %all-to-all-start.5) | async-done | bytes 294944 | tf_op jit(solution)/shard_map/all_to_all | solution.py:612
  38.6 0.8 finish_rows.1
  39.4 7.2 %all-to-all-start.6 = ((bf16[8,16,640]{2,1,0:T(8,128)(2,1)}), bf16[8,16,640]{2,1,0:T(8,128)(2,1)S(1)}, u32[]{:S(2)}, u32[]{:S(2)}) async-start(bf16[8,16,640]{2,1,0:T(8,128)(2,1)} %finish_rows.1), calls=%async_computation.6 | async-start | bytes 327680 | tf_op jit(solution)/shard_map/all_to_all | solution.py:633
  46.7 3.5 %place_rows.1 = (s32[128,128]{1,0:T(8,128)S(1)}, f32[8,128]{1,0:T(8,128)S(1)}, s32[1,1]{1,0:T(1,128)}) custom-call(s32[5]{0:T(128)S(1)} %stack.23.place, s32[104,128]{1,0:T(8,128)S(1)} %rank_rows.1.sheet), custom_call_target="tpu_custom_call" | custom-call | flops 1000000000 | bytes 1000000 | tf_op jit(solution)/shard_map/place_rows/pallas_call | solution.py:635
  50.1 4.5 %all-to-all-done.6 = bf16[8,16,640]{2,1,0:T(8,128)(2,1)S(1)} async-done(((bf16[8,16,640]{2,1,0:T(8,128)(2,1)}), bf16[8,16,640]{2,1,0:T(8,128)(2,1)S(1)}, u32[]{:S(2)}, u32[]{:S(2)}) %all-to-all-start.6) | async-done | bytes 163872 | tf_op jit(solution)/shard_map/all_to_all | solution.py:633
  54.6 1.2 %keep_rows.1 = bf16[16,48,640]{2,1,0:T(8,128)(2,1)} custom-call(f32[8,128]{1,0:T(8,128)S(1)} %get-tuple-element.70.kept, bf16[128,640]{1,0:T(8,128)(2,1)S(1)} %bitcast.56), custom_call_target="tpu_custom_call" | custom-call | tf_op jit(solution)/shard_map/keep_rows/pallas_call | solution.py:651
  55.8 5.4 %all-to-all-start.7 = ((bf16[16,48,640]{2,1,0:T(8,128)(2,1)}), bf16[16,48,640]{2,1,0:T(8,128)(2,1)S(1)}, u32[]{:S(2)}, u32[]{:S(2)}) async-start(bf16[16,48,640]{2,1,0:T(8,128)(2,1)} %keep_rows.1), calls=%async_computation.7 | async-start | bytes 1966080 | tf_op jit(solution)/shard_map/all_to_all | solution.py:662
  61.3 0.1 convert_element_type.44
  61.3 1.1 %copy.103 = f32[16,64,128]{2,0,1:T(8,128)} copy(f32[16,64,128]{2,1,0:T(8,128)S(1)} %bitcast.72) | data formatting | bytes 1048576 | tf_op jit(solution)/shard_map/reshape | solution.py:665
  62.5 2.8 %copy.102 = bf16[16,64,512]{2,0,1:T(8,128)(2,1)} copy(bf16[16,64,512]{2,1,0:T(8,128)(2,1)} %bitcast.67) | data formatting | bytes 2097152 | tf_op jit(solution)/shard_map/reshape | solution.py:665
  65.3 2.0 %copy.99 = bf16[128,8,576]{2,1,0:T(8,128)(2,1)} copy(bf16[128,8,576]{0,2,1:T(8,128)(2,1)S(1)} %copy-done.4) | data formatting | bytes 2359296 | tf_op jit(solution)/shard_map/optimization_barrier | solution.py:659
  67.3 1.6 %copy.100 = bf16[2,8,64,576]{3,2,1,0:T(8,128)(2,1)S(1)} copy(bf16[2,8,64,576]{3,1,0,2:T(8,128)(2,1)} %bitcast.60) | data formatting | bytes 2359296 | tf_op jit(solution)/shard_map/transpose | solution.py:670
  68.9 3.1 %copy.101 = bf16[16,64,576]{2,0,1:T(8,128)(2,1)} copy(bf16[16,64,576]{2,1,0:T(8,128)(2,1)} %bitcast.62) | data formatting | bytes 2359296 | tf_op jit(solution)/shard_map/reshape | solution.py:665
  72.1 0.1 multiply_cosine_fusion.2
  72.3 2.1 %all-to-all-done.7 = bf16[16,48,640]{2,1,0:T(8,128)(2,1)S(1)} async-done(((bf16[16,48,640]{2,1,0:T(8,128)(2,1)}), bf16[16,48,640]{2,1,0:T(8,128)(2,1)S(1)}, u32[]{:S(2)}, u32[]{:S(2)}) %all-to-all-start.7) | async-done | bytes 983072 | tf_op jit(solution)/shard_map/all_to_all | solution.py:662
  74.9 0.2 conditional.1
  75.2 0.4 copy-done
  75.6 2.6 %near_keys.1.near = bf16[2176,640]{1,0:T(8,128)(2,1)S(1)} custom-call(s32[5]{0:T(128)S(1)} %stack.23.place, s32[2]{0:T(128)S(1)} %copy-done, bf16[768,640]{1,0:T(8,128)(2,1)S(1)} %bitcast.55, s32[128,128]{1,0:T(8,128)S(1)} %get-tuple-element.81.columns), custom_call_target="tpu_custom_call" | custom-call | flops 2000000000 | bytes 1000000 | tf_op jit(solution)/shard_map/near_keys/pallas_call | solution.py:695
  78.2 11.6 %decode_rows.1 = bf16[128,4096]{1,0:T(8,128)(2,1)} custom-call(s32[5]{0:T(128)S(1)} %stack.23.place, s32[2]{0:T(128)S(1)} %copy-done, s32[1,1]{1,0:T(1,128)} %get-tuple-element.69.fits, bf16[2176,640]{1,0:T(8,128)(2,1)S(1)} %near_keys.1.near, bf16[768,640]{1,0:T(8,128)(2,1)S(1)} %collective-permute-done.others, s32[128,128]{1,0:T(8,128)S(1)} %get-tuple-element.81.columns, ...), custom_call_target="tpu_custom_call" | custom-call | flops 5000000000 | bytes 7000000 | tf_op jit(solution)/shard_map/decode_rows/pallas_call | solution.py:706
  89.8 3.6 %all-to-all-start.8 = ((bf16[8,16,4096]{2,1,0:T(8,128)(2,1)}), bf16[8,16,4096]{2,1,0:T(8,128)(2,1)S(1)}, u32[]{:S(2)}, u32[]{:S(2)}) async-start(bf16[8,16,4096]{2,1,0:T(8,128)(2,1)} %bitcast.68), calls=%async_computation.8 | async-start | bytes 2097152 | tf_op jit(solution)/shard_map/all_to_all | solution.py:733
  93.4 1.0 copy-done.1
  94.4 1.8 %copy-done.3 = bf16[2176,640]{1,0:T(8,128)(2,1)S(1)} copy-done((bf16[2176,640]{1,0:T(8,128)(2,1)S(1)}, bf16[2176,640]{1,0:T(8,128)(2,1)}, u32[]{:S(2)}) %copy-start.3) | copy-done | bytes 2785304
  96.2 2.1 %prefill_rows.1.prefilled = bf16[128,4096]{1,0:T(8,128)(2,1)} custom-call(s32[5]{0:T(128)S(1)} %stack.23.place, s32[1,1]{1,0:T(1,128)} %get-tuple-element.69.fits, bf16[2176,640]{1,0:T(8,128)(2,1)S(1)} %copy-done.3, bf16[768,640]{1,0:T(8,128)(2,1)S(1)} %collective-permute-done.others, s32[128,128]{1,0:T(8,128)S(1)} %get-tuple-element.81.columns, ...), custom_call_target="tpu_custom_call" | custom-call | flops 7000000000 | bytes 7000000 | tf_op jit(solution)/shard_map/prefill_rows/pallas_call | solution.py:734
  98.3 11.0 %all-to-all-done.8 = bf16[8,16,4096]{2,1,0:T(8,128)(2,1)S(1)} async-done(((bf16[8,16,4096]{2,1,0:T(8,128)(2,1)}), bf16[8,16,4096]{2,1,0:T(8,128)(2,1)S(1)}, u32[]{:S(2)}, u32[]{:S(2)}) %all-to-all-start.8) | async-done | bytes 1048608 | tf_op jit(solution)/shard_map/all_to_all | solution.py:733
  109.3 1.5 %join_rows.1 = bf16[128,4096]{1,0:T(8,128)(2,1)} custom-call(s32[5]{0:T(128)S(1)} %stack.23.place, bf16[128,4096]{1,0:T(8,128)(2,1)} %prefill_rows.1.prefilled, bf16[128,4096]{1,0:T(8,128)(2,1)S(1)} %bitcast.52), custom_call_target="tpu_custom_call", output_to_operand_aliasing={{}: (1, {})} | custom-call | tf_op jit(solution)/shard_map/join_rows/pallas_call | solution.py:750
  (25 shorter events, 0.2 us)
Async XLA Ops:
  1.3 20.2 %all-to-all-start.4 = ((s32[32,1,128]{2,1,0:T(1,128)}), s32[32,1,128]{2,1,0:T(1,128)S(1)}, u32[]{:S(2)}, u32[]{:S(2)}) async-start(s32[32,1,128]{2,1,0:T(1,128)} %spread_ids.1), calls=%async_computation.4 | async-start | bytes 32768 | tf_op jit(solution)/shard_map/all_to_all | solution.py:572
  26.1 12.6 %copy-start.6 = (f32[512]{0:T(512)S(1)}, f32[512]{0:T(512)}, u32[]{:S(2)}) copy-start(f32[512]{0:T(512)} %param.18) | copy-start | bytes 6148
  26.1 12.6 %all-to-all-start.5 = ((f32[8,16,576]{2,1,0:T(8,128)}), f32[8,16,576]{2,1,0:T(8,128)S(1)}, u32[]{:S(2)}, u32[]{:S(2)}) async-start(f32[8,16,576]{2,1,0:T(8,128)} %select_rows.1), calls=%async_computation.5 | async-start | bytes 655360 | tf_op jit(solution)/shard_map/all_to_all | solution.py:612
  35.3 25.9 %copy-start.7 = (s32[8]{0:T(128)S(1)}, s32[8]{0:T(128)}, u32[]{:S(2)}) copy-start(s32[8]{0:T(128)} %lengths.1) | copy-start | bytes 100
  35.3 26.0 %copy-start.5 = (f32[1024,128]{1,0:T(8,128)S(1)}, f32[1024,128]{1,0:T(8,128)}, u32[]{:S(2)}) copy-start(f32[1024,128]{1,0:T(8,128)} %get-tuple-element.78) | copy-start | bytes 1572868
  39.4 15.2 %all-to-all-start.6 = ((bf16[8,16,640]{2,1,0:T(8,128)(2,1)}), bf16[8,16,640]{2,1,0:T(8,128)(2,1)S(1)}, u32[]{:S(2)}, u32[]{:S(2)}) async-start(bf16[8,16,640]{2,1,0:T(8,128)(2,1)} %finish_rows.1), calls=%async_computation.6 | async-start | bytes 327680 | tf_op jit(solution)/shard_map/all_to_all | solution.py:633
  46.7 18.7 %copy-start.4 = (bf16[128,8,576]{0,2,1:T(8,128)(2,1)S(1)}, bf16[128,8,576]{0,2,1:T(8,128)(2,1)}, u32[]{:S(2)}) copy-start(bf16[128,8,576]{0,2,1:T(8,128)(2,1)} %param.19) | copy-start | bytes 3538948
  55.8 18.5 %all-to-all-start.7 = ((bf16[16,48,640]{2,1,0:T(8,128)(2,1)}), bf16[16,48,640]{2,1,0:T(8,128)(2,1)S(1)}, u32[]{:S(2)}, u32[]{:S(2)}) async-start(bf16[16,48,640]{2,1,0:T(8,128)(2,1)} %keep_rows.1), calls=%async_computation.7 | async-start | bytes 1966080 | tf_op jit(solution)/shard_map/all_to_all | solution.py:662
  62.5 9.6 %copy-start.10 = (f32[32]{0:T(128)S(1)}, f32[32]{0:T(128)}, u32[]{:S(2)}) copy-start(f32[32]{0:T(128)} %constant.99) | copy-start | bytes 388
  62.5 12.4 %copy-start.8 = (f32[1,32]{1,0:T(1,128)S(1)}, f32[1,32]{1,0:T(1,128)}, u32[]{:S(2)}) copy-start(f32[1,32]{1,0:T(1,128)} %constant.89.clone) | copy-start | bytes 388
  62.5 12.4 %copy-start.9 = (s32[1,128]{1,0:T(1,128)S(1)}, s32[1,128]{1,0:T(1,128)}, u32[]{:S(2)}) copy-start(s32[1,128]{1,0:T(1,128)} %ids.1) | copy-start | bytes 1540
  74.3 3.8 %collective-permute-start = (bf16[768,640]{1,0:T(8,128)(2,1)S(1)}, bf16[768,640]{1,0:T(8,128)(2,1)S(1)}, u32[]{:S(2)}, u32[]{:S(2)}) collective-permute-start(bf16[768,640]{1,0:T(8,128)(2,1)S(1)} %bitcast.54), channel_id=1, source_target_pairs={{0,2},{2,0},{1,3},{3,1},{4,6},{6,4},{5,7},{7,5},{8,10},{10,8},{9,1... | collective-permute-start | bytes 2949128 | tf_op jit(solution)/shard_map/ppermute | solution.py:674
  74.9 0.7 copy-start
  78.1 11.6 %copy-start.2 = (bf16[2176,640]{1,0:T(8,128)(2,1)}, bf16[2176,640]{1,0:T(8,128)(2,1)S(1)}, u32[]{:S(2)}) copy-start(bf16[2176,640]{1,0:T(8,128)(2,1)S(1)} %near_keys.1.near) | copy-start | bytes 8355844
  89.8 19.5 %all-to-all-start.8 = ((bf16[8,16,4096]{2,1,0:T(8,128)(2,1)}), bf16[8,16,4096]{2,1,0:T(8,128)(2,1)S(1)}, u32[]{:S(2)}, u32[]{:S(2)}) async-start(bf16[8,16,4096]{2,1,0:T(8,128)(2,1)} %bitcast.68), calls=%async_computation.8 | async-start | bytes 2097152 | tf_op jit(solution)/shard_map/all_to_all | solution.py:733
  93.4 1.0 copy-start.1
  94.4 1.8 %copy-start.3 = (bf16[2176,640]{1,0:T(8,128)(2,1)S(1)}, bf16[2176,640]{1,0:T(8,128)(2,1)}, u32[]{:S(2)}) copy-start(bf16[2176,640]{1,0:T(8,128)(2,1)} %copy-done.2) | copy-start | bytes 8355844
where the time goes:
time: 111 us
  Pallas kernels  43.1 us (39%)
  starting transfers between devices  31.5 us (28%)
  waiting for transfers between devices  20.8 us (19%)
  local copies, waits for them, and re-layouts  14.1 us (13%)
    pallas_call x1, Pallas kernels, shards(): pl.pallas_call(decode_kernel, out_shape=pltpu.HBM((128, 4096), bf16), in_...  11.6 us
    all_to_all x1, starting transfers between devices, shards(): every = lax.all_to_all(spread, HOLDERS, 0, 0, tiled=True).reshape(32, 128)  11 us
    all_to_all x1, waiting for transfers between devices, shards(): lax.all_to_all(decoded.reshape(8, 16, 4096), TP, 0, 0, tiled=True)  11 us
    pallas_call x1, Pallas kernels, shards(): pl.pallas_call(cache_kernel, grid_spec=pltpu.PrefetchScalarGridSpec(num_s...  9.07 us
    all_to_all x1, starting transfers between devices, shards(): arrived = lax.all_to_all(sent, 'z', 0, 0, tiled=True)  7.25 us
    reshape x3, local copies, waits for them, and re-layouts, by_head(): return jnp.transpose(rows.reshape(16, 64, -1), (1, 0, 2)).reshape(1024, -1)  7.1 us
    all_to_all x1, starting transfers between devices, shards(): slots = lax.all_to_all(handed, PLANE, 0, 0, tiled=True).reshape(SIDE, WIDE)  5.38 us
    pallas_call x1, Pallas kernels, shards(): pl.pallas_call(rank_kernel, out_shape=shaped((104, 128), jnp.int32), in_s...  4.93 us
  transfers between devices with their start and end apart: 6, of which 4 were waited for; matrix products, arithmetic and copies ran while one was open for 10% of the time, Pallas kernels for 20%

commit v1 on v0

--- a/solution.py
+++ b/solution.py
@@ -280,10 +280,15 @@
     level[...] = jnp.broadcast_to(highest + jnp.log2(total), level.shape)
 
 
-def hot_rows(hot, columns, prompt, side):
+def hot_rows(hot, columns, prompt, side, part):
     turned = pltpu.roll(columns[...], (128 - prompt * 8) % 128, 1) - side * SIDE
-    for block in range(8):
+    for block in range(part * 4, part * 4 + 4):
         hot[block * 128 : (block + 1) * 128, :] = ones_where(iota((128, SIDE), 1) == turned[:, block : block + 1])
+    return hot[part * 512 : (part + 1) * 512, :]
+
+
+def fresh_hot(columns, side):
+    return ones_where(iota((128, SIDE), 1) == columns[:, 18:19] - side * SIDE)
 
 
 def empty_kernel(*refs):
@@ -324,12 +329,9 @@
     def open_prompt(prompt):
         @pl.when((place[4] == 0) | (owner[prompt] == group))
         def _():
-            hot_rows(hot, columns, prompt, 0)
-
-            def open_part(part):
-                near[aligned(prompt * 2 + part, 512), :] = dot(hot[aligned(part, 512), :], slots[...]).astype(bf16)
-
-            whole_loop(2, open_part, 2)
+            for part in range(2):
+                some = hot_rows(hot, columns, prompt, 0, part)
+                near[aligned(prompt * 2 + part, 512), :] = dot(some, slots[...]).astype(bf16)
 
     whole_loop(2, open_prompt)
 
@@ -352,37 +354,26 @@
         for load in loads:
             load.start()
 
-        @pl.when(fitting)
-        def _():
-            span = slice(KEYS, KEYS + 128)
-            found = near[span, :].astype(f32) + dot(fresh_hot(columns, 1), others[...])
-            put_keys(keys, span, found, new_factors[...])
+        span = slice(KEYS, KEYS + 128)
+        found = near[span, :].astype(f32) + dot(fresh_hot(columns, 1), others[...])
+        put_keys(keys, span, found, new_factors[...])
+        loads[0].wait()
+
+        def open_prompt(prompt):
+            @pl.when(owner[prompt] == group)
+            def _():
+                for part in range(2):
+                    span = aligned(prompt * 2 + part, 512)
+                    found = near[span, :].astype(f32) + dot(hot_rows(hot, columns, prompt, 1, part), others[...])
+                    put_keys(keys, span, found, factors[part * 512 : (part + 1) * 512, :])
+
+        whole_loop(2, open_prompt)
 
         @pl.when(jnp.logical_not(fitting))
         def _():
+            copy_in(spare, keys.at[pl.ds(0, KEYS)], sem)
             copy_in(spare_new, keys.at[pl.ds(KEYS, 128)], sem)
 
-        loads[0].wait()
-
-        def open_prompt(prompt):
-            owned = owner[prompt] == group
-
-            @pl.when(owned & fitting)
-            def _():
-                hot_rows(hot, columns, prompt, 1)
-
-                def open_part(part):
-                    span = aligned(prompt * 2 + part, 512)
-                    found = near[span, :].astype(f32) + dot(hot[aligned(part, 512), :], others[...])
-                    put_keys(keys, span, found, factors[aligned(part, 512), :])
-
-                whole_loop(2, open_part, 2)
-
-            @pl.when(owned & jnp.logical_not(fitting))
-            def _():
-                copy_in(spare.at[pl.ds(prompt * 1024, 1024)], keys.at[pl.ds(prompt * 1024, 1024)], sem)
-
-        whole_loop(2, open_prompt)
         for load in loads[1:]:
             load.wait()
         newest = keys[KEYS : KEYS + 128, :]
@@ -438,16 +429,11 @@
     @pl.when(place[4] == 0)
     def _():
         def add_prompt(prompt):
-            @pl.when(fitting)
-            def _():
-                hot_rows(hot, columns, prompt, 1)
-
-                def open_part(part):
-                    span = aligned(part, 512)
-                    found = near[aligned(prompt * 2 + part, 512), :].astype(f32) + dot(hot[span, :], others[...])
-                    put_keys(keys, span, found, factors[span, :])
-
-                whole_loop(2, open_part, 2)
+            for part in range(2):
+                span = slice(part * 512, (part + 1) * 512)
+                found = near[aligned(prompt * 2 + part, 512), :].astype(f32)
+                found = found + dot(hot_rows(hot, columns, prompt, 1, part), others[...])
+                put_keys(keys, span, found, factors[span, :])
 
             @pl.when(jnp.logical_not(fitting))
             def _():

time: 111 us -> 111 us (level)
  the two profiles are of different devices: /device:TPU:56 before, /device:TPU:16 now
where the time goes in v1:
time: 111 us
  Pallas kernels  43 us (39%)
  starting transfers between devices  31.5 us (28%)
  waiting for transfers between devices  21.3 us (19%)
  local copies, waits for them, and re-layouts  14.1 us (13%)
    pallas_call x1, Pallas kernels, shards(): pl.pallas_call(decode_kernel, out_shape=pltpu.HBM((128, 4096), bf16), in_...  11.6 us
    all_to_all x1, starting transfers between devices, shards(): every = lax.all_to_all(spread, HOLDERS, 0, 0, tiled=True).reshape(32, 128)  11.6 us
    all_to_all x1, waiting for transfers between devices, shards(): lax.all_to_all(decoded.reshape(8, 16, 4096), TP, 0, 0, tiled=True)  11 us
    pallas_call x1, Pallas kernels, shards(): pl.pallas_call(cache_kernel, grid_spec=pltpu.PrefetchScalarGridSpec(num_s...  9.07 us
    reshape x3, local copies, waits for them, and re-layouts, by_head(): return jnp.transpose(rows.reshape(16, 64, -1), (1, 0, 2)).reshape(1024, -1)  7.1 us
    all_to_all x1, starting transfers between devices, shards(): arrived = lax.all_to_all(sent, 'z', 0, 0, tiled=True)  6.65 us
    all_to_all x1, waiting for transfers between devices, shards(): arrived = lax.all_to_all(sent, 'z', 0, 0, tiled=True)  5.96 us
    all_to_all x1, starting transfers between devices, shards(): slots = lax.all_to_all(handed, PLANE, 0, 0, tiled=True).reshape(SIDE, WIDE)  5.42 us
  transfers between devices with their start and end apart: 6, of which 4 were waited for; matrix products, arithmetic and copies ran while one was open for 10% of the time, Pallas kernels for 20%

profile of v1, /device:TPU:16, one launch (start us, length us, event | category | flops | bytes accessed | tf_op | source)
XLA Modules:
  0.0 111.4 jit_solution(14045280801007001566)
XLA Ops:
  0.0 1.3 %spread_ids.1 = s32[32,1,128]{2,1,0:T(1,128)} custom-call(s32[1,128]{1,0:T(1,128)} %ids.1), custom_call_target="tpu_custom_call" | custom-call | tf_op jit(solution)/shard_map/spread_ids/pallas_call | solution.py:550
  1.3 11.6 %all-to-all-start.4 = ((s32[32,1,128]{2,1,0:T(1,128)}), s32[32,1,128]{2,1,0:T(1,128)S(1)}, u32[]{:S(2)}, u32[]{:S(2)}) async-start(s32[32,1,128]{2,1,0:T(1,128)} %spread_ids.1), calls=%async_computation.4 | async-start | bytes 32768 | tf_op jit(solution)/shard_map/all_to_all | solution.py:558
  12.9 9.1 %cache_rows.1 = (bf16[1024,512]{1,0:T(8,128)(2,1)}, f32[1024,128]{1,0:T(8,128)}) custom-call(s32[8]{0:T(128)} %lengths.1, bf16[8,128,576]{2,1,0:T(8,128)(2,1)} %bitcast.61, bf16[8,576,512]{2,1,0:T(8,128)(2,1)} %bitcast.63), custom_call_target="tpu_custom_call" | custom-call | flops 1200000000 | bytes 7000000 | tf_op jit(solution)/shard_map/cache_rows/pallas_call | solution.py:560
  21.9 0.1 stack.23.place
  22.0 4.6 %select_rows.1 = f32[8,16,576]{2,1,0:T(8,128)} custom-call(s32[5]{0:T(128)S(1)} %stack.23.place, s32[32,128]{1,0:T(8,128)S(1)} %bitcast.57, bf16[2048,896]{1,0:T(8,128)(2,1)} %table.1, bf16[576,896]{1,0:T(8,128)(2,1)} %bitcast.69), custom_call_target="tpu_custom_call" | custom-call | flops 3000000000 | bytes 5000000 | tf_op jit(solution)/shard_map/select_rows/pallas_call | solution.py:581
  26.6 4.3 %all-to-all-start.5 = ((f32[8,16,576]{2,1,0:T(8,128)}), f32[8,16,576]{2,1,0:T(8,128)S(1)}, u32[]{:S(2)}, u32[]{:S(2)}) async-start(f32[8,16,576]{2,1,0:T(8,128)} %select_rows.1), calls=%async_computation.5 | async-start | bytes 655360 | tf_op jit(solution)/shard_map/all_to_all | solution.py:598
  30.9 4.9 %rank_rows.1.sheet = s32[104,128]{1,0:T(8,128)S(1)} custom-call(s32[32,128]{1,0:T(8,128)S(1)} %bitcast.58), custom_call_target="tpu_custom_call" | custom-call | flops 2000000000 | bytes 1000000 | tf_op jit(solution)/shard_map/rank_rows/pallas_call | solution.py:600
  35.9 3.3 %all-to-all-done.5.parts = f32[8,16,576]{2,1,0:T(8,128)S(1)} async-done(((f32[8,16,576]{2,1,0:T(8,128)}), f32[8,16,576]{2,1,0:T(8,128)S(1)}, u32[]{:S(2)}, u32[]{:S(2)}) %all-to-all-start.5) | async-done | bytes 294944 | tf_op jit(solution)/shard_map/all_to_all | solution.py:598
  39.2 0.8 finish_rows.1
  40.0 6.6 %all-to-all-start.6 = ((bf16[8,16,640]{2,1,0:T(8,128)(2,1)}), bf16[8,16,640]{2,1,0:T(8,128)(2,1)S(1)}, u32[]{:S(2)}, u32[]{:S(2)}) async-start(bf16[8,16,640]{2,1,0:T(8,128)(2,1)} %finish_rows.1), calls=%async_computation.6 | async-start | bytes 327680 | tf_op jit(solution)/shard_map/all_to_all | solution.py:619
  46.6 3.5 %place_rows.1 = (s32[128,128]{1,0:T(8,128)S(1)}, f32[8,128]{1,0:T(8,128)S(1)}, s32[1,1]{1,0:T(1,128)}) custom-call(s32[5]{0:T(128)S(1)} %stack.23.place, s32[104,128]{1,0:T(8,128)S(1)} %rank_rows.1.sheet), custom_call_target="tpu_custom_call" | custom-call | flops 1000000000 | bytes 1000000 | tf_op jit(solution)/shard_map/place_rows/pallas_call | solution.py:621
  50.1 6.0 %all-to-all-done.6 = bf16[8,16,640]{2,1,0:T(8,128)(2,1)S(1)} async-done(((bf16[8,16,640]{2,1,0:T(8,128)(2,1)}), bf16[8,16,640]{2,1,0:T(8,128)(2,1)S(1)}, u32[]{:S(2)}, u32[]{:S(2)}) %all-to-all-start.6) | async-done | bytes 163872 | tf_op jit(solution)/shard_map/all_to_all | solution.py:619
  56.0 1.2 %keep_rows.1 = bf16[16,48,640]{2,1,0:T(8,128)(2,1)} custom-call(f32[8,128]{1,0:T(8,128)S(1)} %get-tuple-element.70.kept, bf16[128,640]{1,0:T(8,128)(2,1)S(1)} %bitcast.56), custom_call_target="tpu_custom_call" | custom-call | tf_op jit(solution)/shard_map/keep_rows/pallas_call | solution.py:637
  57.2 5.4 %all-to-all-start.7 = ((bf16[16,48,640]{2,1,0:T(8,128)(2,1)}), bf16[16,48,640]{2,1,0:T(8,128)(2,1)S(1)}, u32[]{:S(2)}, u32[]{:S(2)}) async-start(bf16[16,48,640]{2,1,0:T(8,128)(2,1)} %keep_rows.1), calls=%async_computation.7 | async-start | bytes 1966080 | tf_op jit(solution)/shard_map/all_to_all | solution.py:648
  62.7 0.1 convert_element_type.44
  62.8 1.1 %copy.103 = f32[16,64,128]{2,0,1:T(8,128)} copy(f32[16,64,128]{2,1,0:T(8,128)S(1)} %bitcast.72) | data formatting | bytes 1048576 | tf_op jit(solution)/shard_map/reshape | solution.py:651
  63.9 2.8 %copy.102 = bf16[16,64,512]{2,0,1:T(8,128)(2,1)} copy(bf16[16,64,512]{2,1,0:T(8,128)(2,1)} %bitcast.67) | data formatting | bytes 2097152 | tf_op jit(solution)/shard_map/reshape | solution.py:651
  66.8 2.0 %copy.99 = bf16[128,8,576]{2,1,0:T(8,128)(2,1)} copy(bf16[128,8,576]{0,2,1:T(8,128)(2,1)S(1)} %copy-done.4) | data formatting | bytes 2359296 | tf_op jit(solution)/shard_map/optimization_barrier | solution.py:645
  68.8 1.6 %copy.100 = bf16[2,8,64,576]{3,2,1,0:T(8,128)(2,1)S(1)} copy(bf16[2,8,64,576]{3,1,0,2:T(8,128)(2,1)} %bitcast.60) | data formatting | bytes 2359296 | tf_op jit(solution)/shard_map/transpose | solution.py:656
  70.4 3.1 %copy.101 = bf16[16,64,576]{2,0,1:T(8,128)(2,1)} copy(bf16[16,64,576]{2,1,0:T(8,128)(2,1)} %bitcast.62) | data formatting | bytes 2359296 | tf_op jit(solution)/shard_map/reshape | solution.py:651
  73.5 0.1 multiply_cosine_fusion.2
  73.7 1.1 all-to-all-done.7
  75.4 0.2 conditional.1
  75.7 0.4 copy-done
  76.1 2.5 %near_keys.1.near = bf16[2176,640]{1,0:T(8,128)(2,1)S(1)} custom-call(s32[5]{0:T(128)S(1)} %stack.23.place, s32[2]{0:T(128)S(1)} %copy-done, bf16[768,640]{1,0:T(8,128)(2,1)S(1)} %bitcast.55, s32[128,128]{1,0:T(8,128)S(1)} %get-tuple-element.81.columns), custom_call_target="tpu_custom_call" | custom-call | flops 2000000000 | bytes 1000000 | tf_op jit(solution)/shard_map/near_keys/pallas_call | solution.py:681
  78.6 11.6 %decode_rows.1 = bf16[128,4096]{1,0:T(8,128)(2,1)} custom-call(s32[5]{0:T(128)S(1)} %stack.23.place, s32[2]{0:T(128)S(1)} %copy-done, s32[1,1]{1,0:T(1,128)} %get-tuple-element.69.fits, bf16[2176,640]{1,0:T(8,128)(2,1)S(1)} %near_keys.1.near, bf16[768,640]{1,0:T(8,128)(2,1)S(1)} %collective-permute-done.others, s32[128,128]{1,0:T(8,128)S(1)} %get-tuple-element.81.columns, ...), custom_call_target="tpu_custom_call" | custom-call | flops 5000000000 | bytes 7000000 | tf_op jit(solution)/shard_map/decode_rows/pallas_call | solution.py:692
  90.2 3.6 %all-to-all-start.8 = ((bf16[8,16,4096]{2,1,0:T(8,128)(2,1)}), bf16[8,16,4096]{2,1,0:T(8,128)(2,1)S(1)}, u32[]{:S(2)}, u32[]{:S(2)}) async-start(bf16[8,16,4096]{2,1,0:T(8,128)(2,1)} %bitcast.68), calls=%async_computation.8 | async-start | bytes 2097152 | tf_op jit(solution)/shard_map/all_to_all | solution.py:719
  93.8 1.0 copy-done.1
  94.8 1.8 %copy-done.3 = bf16[2176,640]{1,0:T(8,128)(2,1)S(1)} copy-done((bf16[2176,640]{1,0:T(8,128)(2,1)S(1)}, bf16[2176,640]{1,0:T(8,128)(2,1)}, u32[]{:S(2)}) %copy-start.3) | copy-done | bytes 2785304
  96.6 2.1 %prefill_rows.1.prefilled = bf16[128,4096]{1,0:T(8,128)(2,1)} custom-call(s32[5]{0:T(128)S(1)} %stack.23.place, s32[1,1]{1,0:T(1,128)} %get-tuple-element.69.fits, bf16[2176,640]{1,0:T(8,128)(2,1)S(1)} %copy-done.3, bf16[768,640]{1,0:T(8,128)(2,1)S(1)} %collective-permute-done.others, s32[128,128]{1,0:T(8,128)S(1)} %get-tuple-element.81.columns, ...), custom_call_target="tpu_custom_call" | custom-call | flops 7000000000 | bytes 7000000 | tf_op jit(solution)/shard_map/prefill_rows/pallas_call | solution.py:720
  98.7 11.0 %all-to-all-done.8 = bf16[8,16,4096]{2,1,0:T(8,128)(2,1)S(1)} async-done(((bf16[8,16,4096]{2,1,0:T(8,128)(2,1)}), bf16[8,16,4096]{2,1,0:T(8,128)(2,1)S(1)}, u32[]{:S(2)}, u32[]{:S(2)}) %all-to-all-start.8) | async-done | bytes 1048608 | tf_op jit(solution)/shard_map/all_to_all | solution.py:719
  109.7 1.5 %join_rows.1 = bf16[128,4096]{1,0:T(8,128)(2,1)} custom-call(s32[5]{0:T(128)S(1)} %stack.23.place, bf16[128,4096]{1,0:T(8,128)(2,1)} %prefill_rows.1.prefilled, bf16[128,4096]{1,0:T(8,128)(2,1)S(1)} %bitcast.52), custom_call_target="tpu_custom_call", output_to_operand_aliasing={{}: (1, {})} | custom-call | tf_op jit(solution)/shard_map/join_rows/pallas_call | solution.py:736
  (25 shorter events, 0.2 us)
Async XLA Ops:
  1.3 20.8 %all-to-all-start.4 = ((s32[32,1,128]{2,1,0:T(1,128)}), s32[32,1,128]{2,1,0:T(1,128)S(1)}, u32[]{:S(2)}, u32[]{:S(2)}) async-start(s32[32,1,128]{2,1,0:T(1,128)} %spread_ids.1), calls=%async_computation.4 | async-start | bytes 32768 | tf_op jit(solution)/shard_map/all_to_all | solution.py:558
  26.6 12.6 %copy-start.6 = (f32[512]{0:T(512)S(1)}, f32[512]{0:T(512)}, u32[]{:S(2)}) copy-start(f32[512]{0:T(512)} %param.18) | copy-start | bytes 6148
  26.6 12.6 %all-to-all-start.5 = ((f32[8,16,576]{2,1,0:T(8,128)}), f32[8,16,576]{2,1,0:T(8,128)S(1)}, u32[]{:S(2)}, u32[]{:S(2)}) async-start(f32[8,16,576]{2,1,0:T(8,128)} %select_rows.1), calls=%async_computation.5 | async-start | bytes 655360 | tf_op jit(solution)/shard_map/all_to_all | solution.py:598
  35.9 26.8 %copy-start.7 = (s32[8]{0:T(128)S(1)}, s32[8]{0:T(128)}, u32[]{:S(2)}) copy-start(s32[8]{0:T(128)} %lengths.1) | copy-start | bytes 100
  35.9 26.9 %copy-start.5 = (f32[1024,128]{1,0:T(8,128)S(1)}, f32[1024,128]{1,0:T(8,128)}, u32[]{:S(2)}) copy-start(f32[1024,128]{1,0:T(8,128)} %get-tuple-element.78) | copy-start | bytes 1572868
  40.0 16.1 %all-to-all-start.6 = ((bf16[8,16,640]{2,1,0:T(8,128)(2,1)}), bf16[8,16,640]{2,1,0:T(8,128)(2,1)S(1)}, u32[]{:S(2)}, u32[]{:S(2)}) async-start(bf16[8,16,640]{2,1,0:T(8,128)(2,1)} %finish_rows.1), calls=%async_computation.6 | async-start | bytes 327680 | tf_op jit(solution)/shard_map/all_to_all | solution.py:619
  46.6 20.2 %copy-start.4 = (bf16[128,8,576]{0,2,1:T(8,128)(2,1)S(1)}, bf16[128,8,576]{0,2,1:T(8,128)(2,1)}, u32[]{:S(2)}) copy-start(bf16[128,8,576]{0,2,1:T(8,128)(2,1)} %param.19) | copy-start | bytes 3538948
  57.2 17.6 %all-to-all-start.7 = ((bf16[16,48,640]{2,1,0:T(8,128)(2,1)}), bf16[16,48,640]{2,1,0:T(8,128)(2,1)S(1)}, u32[]{:S(2)}, u32[]{:S(2)}) async-start(bf16[16,48,640]{2,1,0:T(8,128)(2,1)} %keep_rows.1), calls=%async_computation.7 | async-start | bytes 1966080 | tf_op jit(solution)/shard_map/all_to_all | solution.py:648
  63.9 9.6 %copy-start.10 = (f32[32]{0:T(128)S(1)}, f32[32]{0:T(128)}, u32[]{:S(2)}) copy-start(f32[32]{0:T(128)} %constant.99) | copy-start | bytes 388
  63.9 11.5 %copy-start.8 = (f32[1,32]{1,0:T(1,128)S(1)}, f32[1,32]{1,0:T(1,128)}, u32[]{:S(2)}) copy-start(f32[1,32]{1,0:T(1,128)} %constant.89.clone) | copy-start | bytes 388
  63.9 11.5 %copy-start.9 = (s32[1,128]{1,0:T(1,128)S(1)}, s32[1,128]{1,0:T(1,128)}, u32[]{:S(2)}) copy-start(s32[1,128]{1,0:T(1,128)} %ids.1) | copy-start | bytes 1540
  74.8 3.7 %collective-permute-start = (bf16[768,640]{1,0:T(8,128)(2,1)S(1)}, bf16[768,640]{1,0:T(8,128)(2,1)S(1)}, u32[]{:S(2)}, u32[]{:S(2)}) collective-permute-start(bf16[768,640]{1,0:T(8,128)(2,1)S(1)} %bitcast.54), channel_id=1, source_target_pairs={{0,2},{2,0},{1,3},{3,1},{4,6},{6,4},{5,7},{7,5},{8,10},{10,8},{9,1... | collective-permute-start | bytes 2949128 | tf_op jit(solution)/shard_map/ppermute | solution.py:660
  75.4 0.7 copy-start
  78.5 11.7 %copy-start.2 = (bf16[2176,640]{1,0:T(8,128)(2,1)}, bf16[2176,640]{1,0:T(8,128)(2,1)S(1)}, u32[]{:S(2)}) copy-start(bf16[2176,640]{1,0:T(8,128)(2,1)S(1)} %near_keys.1.near) | copy-start | bytes 8355844
  90.2 19.5 %all-to-all-start.8 = ((bf16[8,16,4096]{2,1,0:T(8,128)(2,1)}), bf16[8,16,4096]{2,1,0:T(8,128)(2,1)S(1)}, u32[]{:S(2)}, u32[]{:S(2)}) async-start(bf16[8,16,4096]{2,1,0:T(8,128)(2,1)} %bitcast.68), calls=%async_computation.8 | async-start | bytes 2097152 | tf_op jit(solution)/shard_map/all_to_all | solution.py:719
  93.8 1.0 copy-start.1
  94.8 1.8 %copy-start.3 = (bf16[2176,640]{1,0:T(8,128)(2,1)S(1)}, bf16[2176,640]{1,0:T(8,128)(2,1)}, u32[]{:S(2)}) copy-start(bf16[2176,640]{1,0:T(8,128)(2,1)} %copy-done.2) | copy-start | bytes 8355844

commit v2 on v1

--- a/solution.py
+++ b/solution.py
@@ -319,7 +319,7 @@
     return new, jnp.exp2(old - new), jnp.sum(weights, axis=-1, keepdims=True), weights.astype(bf16)
 
 
-def near_kernel(place, owner, slots, columns, near, hot):
+def near_kernel(place, slots, columns, near, hot):
     group = place[0] * 8 + place[1]
 
     @pl.when(place[4] == 1)
@@ -327,7 +327,7 @@
         near[KEYS : KEYS + 128, :] = dot(fresh_hot(columns, 0), slots[...]).astype(bf16)
 
     def open_prompt(prompt):
-        @pl.when((place[4] == 0) | (owner[prompt] == group))
+        @pl.when((place[4] == 0) | (place[5 + prompt] == group))
         def _():
             for part in range(2):
                 some = hot_rows(hot, columns, prompt, 0, part)
@@ -337,7 +337,7 @@
 
 
 def decode_kernel(
-    place, owner, fits, near, others, columns, new_factors, factors_far, query_far, earlier_far, level_far, spare, spare_new,
+    place, fits, near, others, columns, new_factors, factors_far, query_far, earlier_far, level_far, spare, spare_new,
     out, out_here, factors, query, earlier, level, keys, hot, highest, total, mixed, sem, in_sems, out_sems
 ):
     group = place[0] * 8 + place[1]
@@ -360,7 +360,7 @@
         loads[0].wait()
 
         def open_prompt(prompt):
-            @pl.when(owner[prompt] == group)
+            @pl.when(place[5 + prompt] == group)
             def _():
                 for part in range(2):
                     span = aligned(prompt * 2 + part, 512)
@@ -393,7 +393,7 @@
         whole_loop(4, begin, 4)
 
         def add_prompt(prompt):
-            @pl.when(owner[prompt] == group)
+            @pl.when(place[5 + prompt] == group)
             def _():
                 def add_part(piece):
                     span = aligned(piece, 256)
@@ -541,6 +541,7 @@
     prompt_owner,
 ):
     place = jnp.stack([lax.axis_index(name) for name in ("ylo", "z", "x", "core", "role")]).astype(jnp.int32)
+    place = jnp.concatenate([place, prompt_owner])
     down = jnp.transpose(latent_down)
     whole = pl.BlockSpec(memory_space=VMEM)
     scalars = pl.BlockSpec(memory_space=SMEM)
@@ -681,18 +682,18 @@
     near = pl.pallas_call(
         near_kernel,
         out_shape=VMEM((KEYS + 128, WIDE), bf16),
-        in_specs=[scalars, scalars, whole, whole],
+        in_specs=[scalars, whole, whole],
         out_specs=whole,
         scratch_shapes=[VMEM((1024, SIDE), bf16)],
         compiler_params=params(12),
         cost_estimate=pl.CostEstimate(flops=2 * 10**9, bytes_accessed=10**6, transcendentals=0),
         name="near_keys",
-    )(place, prompt_owner, slots, columns)
+    )(place, slots, columns)
     factors = jnp.asarray(rope_factors(np.arange(1024, dtype=np.float32)))
     decoded = pl.pallas_call(
         decode_kernel,
         out_shape=pltpu.HBM((128, 4096), bf16),
-        in_specs=[scalars] * 3 + [whole] * 4 + [anywhere] * 6,
+        in_specs=[scalars] * 2 + [whole] * 4 + [anywhere] * 6,
         out_specs=anywhere,
         scratch_shapes=[
             VMEM((128, 4096), bf16),
@@ -713,7 +714,7 @@
         cost_estimate=pl.CostEstimate(flops=5 * 10**9, bytes_accessed=7 * 10**6, transcendentals=10**6),
         name="decode_rows",
     )(
-        place, prompt_owner, fits, in_vmem(near), in_vmem(others), columns, new_factors, in_hbm(factors),
+        place, fits, in_vmem(near), in_vmem(others), columns, new_factors, in_hbm(factors),
         in_hbm(row_query), in_hbm(earlier), in_hbm(level), in_hbm(spare), in_hbm(spare_new),
     )
     turned = lax.all_to_all(decoded.reshape(8, 16, 4096), TP, 0, 0, tiled=True).reshape(128, 4096)

time: 111 us -> 108 us (0.973)
  the two profiles are of different devices: /device:TPU:16 before, /device:TPU:24 now
where the time goes in v2:
time: 108 us; the launch traced here: 106 us
  Pallas kernels  36.3 us (34%)
  starting transfers between devices  31.4 us (29%)
  waiting for transfers between devices  23 us (21%)
  local copies, waits for them, and re-layouts  13.7 us (13%)
    all_to_all x1, starting transfers between devices, shards(): every = lax.all_to_all(spread, HOLDERS, 0, 0, tiled=True).reshape(32, 128)  11.5 us
    all_to_all x1, waiting for transfers between devices, shards(): lax.all_to_all(decoded.reshape(8, 16, 4096), TP, 0, 0, tiled=True)  11 us
    pallas_call x1, Pallas kernels, shards(): pl.pallas_call(cache_kernel, grid_spec=pltpu.PrefetchScalarGridSpec(num_s...  9.07 us
    reshape x3, local copies, waits for them, and re-layouts, by_head(): return jnp.transpose(rows.reshape(16, 64, -1), (1, 0, 2)).reshape(1024, -1)  7.1 us
    all_to_all x1, starting transfers between devices, shards(): arrived = lax.all_to_all(sent, 'z', 0, 0, tiled=True)  6.69 us
    pallas_call x1, Pallas kernels, shards(): pl.pallas_call(decode_kernel, out_shape=pltpu.HBM((128, 4096), bf16), in_...  6.46 us
    all_to_all x1, waiting for transfers between devices, shards(): arrived = lax.all_to_all(sent, 'z', 0, 0, tiled=True)  5.96 us
    all_to_all x1, starting transfers between devices, shards(): slots = lax.all_to_all(handed, PLANE, 0, 0, tiled=True).reshape(SIDE, WIDE)  5.37 us
  transfers between devices with their start and end apart: 6, of which 5 were waited for; matrix products, arithmetic and copies ran while one was open for 10% of the time, Pallas kernels for 19%

profile of v2, /device:TPU:24, one launch (start us, length us, event | category | flops | bytes accessed | tf_op | source)
XLA Modules:
  0.0 105.9 jit_solution(18307357176740187401)
XLA Ops:
  0.0 1.3 %spread_ids.1 = s32[32,1,128]{2,1,0:T(1,128)} custom-call(s32[1,128]{1,0:T(1,128)} %ids.1), custom_call_target="tpu_custom_call" | custom-call | tf_op jit(solution)/shard_map/spread_ids/pallas_call | solution.py:551
  1.3 11.5 %all-to-all-start.4 = ((s32[32,1,128]{2,1,0:T(1,128)}), s32[32,1,128]{2,1,0:T(1,128)S(1)}, u32[]{:S(2)}, u32[]{:S(2)}) async-start(s32[32,1,128]{2,1,0:T(1,128)} %spread_ids.1), calls=%async_computation.4 | async-start | bytes 32768 | tf_op jit(solution)/shard_map/all_to_all | solution.py:559
  12.8 9.1 %cache_rows.1 = (bf16[1024,512]{1,0:T(8,128)(2,1)}, f32[1024,128]{1,0:T(8,128)}) custom-call(s32[8]{0:T(128)} %lengths.1, bf16[8,128,576]{2,1,0:T(8,128)(2,1)} %bitcast.61, bf16[8,576,512]{2,1,0:T(8,128)(2,1)} %bitcast.63), custom_call_target="tpu_custom_call" | custom-call | flops 1200000000 | bytes 7000000 | tf_op jit(solution)/shard_map/cache_rows/pallas_call | solution.py:561
  21.8 0.1 concatenate.41.place
  21.9 4.6 %select_rows.1 = f32[8,16,576]{2,1,0:T(8,128)} custom-call(s32[7]{0:T(128)S(1)} %concatenate.41.place, s32[32,128]{1,0:T(8,128)S(1)} %bitcast.57, bf16[2048,896]{1,0:T(8,128)(2,1)} %table.1, bf16[576,896]{1,0:T(8,128)(2,1)} %bitcast.69), custom_call_target="tpu_custom_call" | custom-call | flops 3000000000 | bytes 5000000 | tf_op jit(solution)/shard_map/select_rows/pallas_call | solution.py:582
  26.5 4.3 %all-to-all-start.5 = ((f32[8,16,576]{2,1,0:T(8,128)}), f32[8,16,576]{2,1,0:T(8,128)S(1)}, u32[]{:S(2)}, u32[]{:S(2)}) async-start(f32[8,16,576]{2,1,0:T(8,128)} %select_rows.1), calls=%async_computation.5 | async-start | bytes 655360 | tf_op jit(solution)/shard_map/all_to_all | solution.py:599
  30.9 4.9 %rank_rows.1.sheet = s32[104,128]{1,0:T(8,128)S(1)} custom-call(s32[32,128]{1,0:T(8,128)S(1)} %bitcast.58), custom_call_target="tpu_custom_call" | custom-call | flops 2000000000 | bytes 1000000 | tf_op jit(solution)/shard_map/rank_rows/pallas_call | solution.py:601
  35.8 3.3 %all-to-all-done.5.parts = f32[8,16,576]{2,1,0:T(8,128)S(1)} async-done(((f32[8,16,576]{2,1,0:T(8,128)}), f32[8,16,576]{2,1,0:T(8,128)S(1)}, u32[]{:S(2)}, u32[]{:S(2)}) %all-to-all-start.5) | async-done | bytes 294944 | tf_op jit(solution)/shard_map/all_to_all | solution.py:599
  39.1 0.8 finish_rows.1
  39.9 6.7 %all-to-all-start.6 = ((bf16[8,16,640]{2,1,0:T(8,128)(2,1)}), bf16[8,16,640]{2,1,0:T(8,128)(2,1)S(1)}, u32[]{:S(2)}, u32[]{:S(2)}) async-start(bf16[8,16,640]{2,1,0:T(8,128)(2,1)} %finish_rows.1), calls=%async_computation.6 | async-start | bytes 327680 | tf_op jit(solution)/shard_map/all_to_all | solution.py:620
  46.6 3.5 %place_rows.1 = (s32[128,128]{1,0:T(8,128)S(1)}, f32[8,128]{1,0:T(8,128)S(1)}, s32[1,1]{1,0:T(1,128)}) custom-call(s32[7]{0:T(128)S(1)} %concatenate.41.place, s32[104,128]{1,0:T(8,128)S(1)} %rank_rows.1.sheet), custom_call_target="tpu_custom_call" | custom-call | flops 1000000000 | bytes 1000000 | tf_op jit(solution)/shard_map/place_rows/pallas_call | solution.py:622
  50.0 6.0 %all-to-all-done.6 = bf16[8,16,640]{2,1,0:T(8,128)(2,1)S(1)} async-done(((bf16[8,16,640]{2,1,0:T(8,128)(2,1)}), bf16[8,16,640]{2,1,0:T(8,128)(2,1)S(1)}, u32[]{:S(2)}, u32[]{:S(2)}) %all-to-all-start.6) | async-done | bytes 163872 | tf_op jit(solution)/shard_map/all_to_all | solution.py:620
  56.0 1.2 %keep_rows.1 = bf16[16,48,640]{2,1,0:T(8,128)(2,1)} custom-call(f32[8,128]{1,0:T(8,128)S(1)} %get-tuple-element.70.kept, bf16[128,640]{1,0:T(8,128)(2,1)S(1)} %bitcast.56), custom_call_target="tpu_custom_call" | custom-call | tf_op jit(solution)/shard_map/keep_rows/pallas_call | solution.py:638
  57.2 5.4 %all-to-all-start.7 = ((bf16[16,48,640]{2,1,0:T(8,128)(2,1)}), bf16[16,48,640]{2,1,0:T(8,128)(2,1)S(1)}, u32[]{:S(2)}, u32[]{:S(2)}) async-start(bf16[16,48,640]{2,1,0:T(8,128)(2,1)} %keep_rows.1), calls=%async_computation.7 | async-start | bytes 1966080 | tf_op jit(solution)/shard_map/all_to_all | solution.py:649
  62.6 0.1 convert_element_type.44
  62.7 1.1 %copy.103 = f32[16,64,128]{2,0,1:T(8,128)} copy(f32[16,64,128]{2,1,0:T(8,128)S(1)} %bitcast.72) | data formatting | bytes 1048576 | tf_op jit(solution)/shard_map/reshape | solution.py:652
  63.8 2.8 %copy.102 = bf16[16,64,512]{2,0,1:T(8,128)(2,1)} copy(bf16[16,64,512]{2,1,0:T(8,128)(2,1)} %bitcast.67) | data formatting | bytes 2097152 | tf_op jit(solution)/shard_map/reshape | solution.py:652
  66.7 2.0 %copy.99 = bf16[128,8,576]{2,1,0:T(8,128)(2,1)} copy(bf16[128,8,576]{0,2,1:T(8,128)(2,1)S(1)} %copy-done.3) | data formatting | bytes 2359296 | tf_op jit(solution)/shard_map/optimization_barrier | solution.py:646
  68.7 1.6 %copy.100 = bf16[2,8,64,576]{3,2,1,0:T(8,128)(2,1)S(1)} copy(bf16[2,8,64,576]{3,1,0,2:T(8,128)(2,1)} %bitcast.60) | data formatting | bytes 2359296 | tf_op jit(solution)/shard_map/transpose | solution.py:657
  70.3 3.1 %copy.101 = bf16[16,64,576]{2,0,1:T(8,128)(2,1)} copy(bf16[16,64,576]{2,1,0:T(8,128)(2,1)} %bitcast.62) | data formatting | bytes 2359296 | tf_op jit(solution)/shard_map/reshape | solution.py:652
  73.4 0.1 multiply_cosine_fusion.2
  73.6 2.1 %all-to-all-done.7 = bf16[16,48,640]{2,1,0:T(8,128)(2,1)S(1)} async-done(((bf16[16,48,640]{2,1,0:T(8,128)(2,1)}), bf16[16,48,640]{2,1,0:T(8,128)(2,1)S(1)}, u32[]{:S(2)}, u32[]{:S(2)}) %all-to-all-start.7) | async-done | bytes 983072 | tf_op jit(solution)/shard_map/all_to_all | solution.py:649
  76.3 0.2 conditional.1
  76.5 0.9 near_keys.1.near
  77.5 0.8 collective-permute-done.others
  78.3 6.5 %decode_rows.1 = bf16[128,4096]{1,0:T(8,128)(2,1)} custom-call(s32[7]{0:T(128)S(1)} %concatenate.41.place, s32[1,1]{1,0:T(1,128)} %get-tuple-element.69.fits, bf16[2176,640]{1,0:T(8,128)(2,1)S(1)} %near_keys.1.near, bf16[768,640]{1,0:T(8,128)(2,1)S(1)} %collective-permute-done.others, s32[128,128]{1,0:T(8,128)S(1)} %get-tuple-element.81.columns, ...), custom_call_target="tpu_custom_call" | custom-call | flops 5000000000 | bytes 7000000 | tf_op jit(solution)/shard_map/decode_rows/pallas_call | solution.py:693
  84.7 3.6 %all-to-all-start.8 = ((bf16[8,16,4096]{2,1,0:T(8,128)(2,1)}), bf16[8,16,4096]{2,1,0:T(8,128)(2,1)S(1)}, u32[]{:S(2)}, u32[]{:S(2)}) async-start(bf16[8,16,4096]{2,1,0:T(8,128)(2,1)} %bitcast.68), calls=%async_computation.8 | async-start | bytes 2097152 | tf_op jit(solution)/shard_map/all_to_all | solution.py:720
  88.3 1.0 copy-done
  89.4 1.8 %copy-done.2 = bf16[2176,640]{1,0:T(8,128)(2,1)S(1)} copy-done((bf16[2176,640]{1,0:T(8,128)(2,1)S(1)}, bf16[2176,640]{1,0:T(8,128)(2,1)}, u32[]{:S(2)}) %copy-start.2) | copy-done | bytes 2785304
  91.1 2.1 %prefill_rows.1.prefilled = bf16[128,4096]{1,0:T(8,128)(2,1)} custom-call(s32[7]{0:T(128)S(1)} %concatenate.41.place, s32[1,1]{1,0:T(1,128)} %get-tuple-element.69.fits, bf16[2176,640]{1,0:T(8,128)(2,1)S(1)} %copy-done.2, bf16[768,640]{1,0:T(8,128)(2,1)S(1)} %collective-permute-done.others, s32[128,128]{1,0:T(8,128)S(1)} %get-tuple-element.81.columns, ...), custom_call_target="tpu_custom_call" | custom-call | flops 7000000000 | bytes 7000000 | tf_op jit(solution)/shard_map/prefill_rows/pallas_call | solution.py:721
  93.2 11.0 %all-to-all-done.8 = bf16[8,16,4096]{2,1,0:T(8,128)(2,1)S(1)} async-done(((bf16[8,16,4096]{2,1,0:T(8,128)(2,1)}), bf16[8,16,4096]{2,1,0:T(8,128)(2,1)S(1)}, u32[]{:S(2)}, u32[]{:S(2)}) %all-to-all-start.8) | async-done | bytes 1048608 | tf_op jit(solution)/shard_map/all_to_all | solution.py:720
  104.2 1.5 %join_rows.1 = bf16[128,4096]{1,0:T(8,128)(2,1)} custom-call(s32[7]{0:T(128)S(1)} %concatenate.41.place, bf16[128,4096]{1,0:T(8,128)(2,1)} %prefill_rows.1.prefilled, bf16[128,4096]{1,0:T(8,128)(2,1)S(1)} %bitcast.52), custom_call_target="tpu_custom_call", output_to_operand_aliasing={{}: (1, {})} | custom-call | tf_op jit(solution)/shard_map/join_rows/pallas_call | solution.py:737
  (25 shorter events, 0.2 us)
Async XLA Ops:
  0.0 21.8 %copy-start.9 = (s32[2]{0:T(128)S(1)}, s32[2]{0:T(128)}, u32[]{:S(2)}) copy-start(s32[2]{0:T(128)} %param.23) | copy-start | bytes 28
  1.3 20.6 %all-to-all-start.4 = ((s32[32,1,128]{2,1,0:T(1,128)}), s32[32,1,128]{2,1,0:T(1,128)S(1)}, u32[]{:S(2)}, u32[]{:S(2)}) async-start(s32[32,1,128]{2,1,0:T(1,128)} %spread_ids.1), calls=%async_computation.4 | async-start | bytes 32768 | tf_op jit(solution)/shard_map/all_to_all | solution.py:559
  26.5 12.6 %copy-start.5 = (f32[512]{0:T(512)S(1)}, f32[512]{0:T(512)}, u32[]{:S(2)}) copy-start(f32[512]{0:T(512)} %param.18) | copy-start | bytes 6148
  26.5 12.6 %all-to-all-start.5 = ((f32[8,16,576]{2,1,0:T(8,128)}), f32[8,16,576]{2,1,0:T(8,128)S(1)}, u32[]{:S(2)}, u32[]{:S(2)}) async-start(f32[8,16,576]{2,1,0:T(8,128)} %select_rows.1), calls=%async_computation.5 | async-start | bytes 655360 | tf_op jit(solution)/shard_map/all_to_all | solution.py:599
  35.8 26.8 %copy-start.6 = (s32[8]{0:T(128)S(1)}, s32[8]{0:T(128)}, u32[]{:S(2)}) copy-start(s32[8]{0:T(128)} %lengths.1) | copy-start | bytes 100
  35.8 26.9 %copy-start.4 = (f32[1024,128]{1,0:T(8,128)S(1)}, f32[1024,128]{1,0:T(8,128)}, u32[]{:S(2)}) copy-start(f32[1024,128]{1,0:T(8,128)} %get-tuple-element.78) | copy-start | bytes 1572868
  39.9 16.1 %all-to-all-start.6 = ((bf16[8,16,640]{2,1,0:T(8,128)(2,1)}), bf16[8,16,640]{2,1,0:T(8,128)(2,1)S(1)}, u32[]{:S(2)}, u32[]{:S(2)}) async-start(bf16[8,16,640]{2,1,0:T(8,128)(2,1)} %finish_rows.1), calls=%async_computation.6 | async-start | bytes 327680 | tf_op jit(solution)/shard_map/all_to_all | solution.py:620
  46.6 20.1 %copy-start.3 = (bf16[128,8,576]{0,2,1:T(8,128)(2,1)S(1)}, bf16[128,8,576]{0,2,1:T(8,128)(2,1)}, u32[]{:S(2)}) copy-start(bf16[128,8,576]{0,2,1:T(8,128)(2,1)} %param.19) | copy-start | bytes 3538948
  57.2 18.5 %all-to-all-start.7 = ((bf16[16,48,640]{2,1,0:T(8,128)(2,1)}), bf16[16,48,640]{2,1,0:T(8,128)(2,1)S(1)}, u32[]{:S(2)}, u32[]{:S(2)}) async-start(bf16[16,48,640]{2,1,0:T(8,128)(2,1)} %keep_rows.1), calls=%async_computation.7 | async-start | bytes 1966080 | tf_op jit(solution)/shard_map/all_to_all | solution.py:649
  63.8 9.6 %copy-start.10 = (f32[32]{0:T(128)S(1)}, f32[32]{0:T(128)}, u32[]{:S(2)}) copy-start(f32[32]{0:T(128)} %constant.99) | copy-start | bytes 388
  63.8 12.4 %copy-start.7 = (f32[1,32]{1,0:T(1,128)S(1)}, f32[1,32]{1,0:T(1,128)}, u32[]{:S(2)}) copy-start(f32[1,32]{1,0:T(1,128)} %constant.89.clone) | copy-start | bytes 388
  63.8 12.4 %copy-start.8 = (s32[1,128]{1,0:T(1,128)S(1)}, s32[1,128]{1,0:T(1,128)}, u32[]{:S(2)}) copy-start(s32[1,128]{1,0:T(1,128)} %ids.1) | copy-start | bytes 1540
  75.7 2.6 %collective-permute-start = (bf16[768,640]{1,0:T(8,128)(2,1)S(1)}, bf16[768,640]{1,0:T(8,128)(2,1)S(1)}, u32[]{:S(2)}, u32[]{:S(2)}) collective-permute-start(bf16[768,640]{1,0:T(8,128)(2,1)S(1)} %bitcast.54), channel_id=1, source_target_pairs={{0,2},{2,0},{1,3},{3,1},{4,6},{6,4},{5,7},{7,5},{8,10},{10,8},{9,1... | collective-permute-start | bytes 2949128 | tf_op jit(solution)/shard_map/ppermute | solution.py:661
  77.5 7.2 %copy-start.1 = (bf16[2176,640]{1,0:T(8,128)(2,1)}, bf16[2176,640]{1,0:T(8,128)(2,1)S(1)}, u32[]{:S(2)}) copy-start(bf16[2176,640]{1,0:T(8,128)(2,1)S(1)} %near_keys.1.near) | copy-start | bytes 8355844
  84.7 19.5 %all-to-all-start.8 = ((bf16[8,16,4096]{2,1,0:T(8,128)(2,1)}), bf16[8,16,4096]{2,1,0:T(8,128)(2,1)S(1)}, u32[]{:S(2)}, u32[]{:S(2)}) async-start(bf16[8,16,4096]{2,1,0:T(8,128)(2,1)} %bitcast.68), calls=%async_computation.8 | async-start | bytes 2097152 | tf_op jit(solution)/shard_map/all_to_all | solution.py:720
  88.3 1.0 copy-start
  89.4 1.8 %copy-start.2 = (bf16[2176,640]{1,0:T(8,128)(2,1)S(1)}, bf16[2176,640]{1,0:T(8,128)(2,1)}, u32[]{:S(2)}) copy-start(bf16[2176,640]{1,0:T(8,128)(2,1)} %copy-done.1) | copy-start | bytes 8355844
